TPU v7x, 32 devices: a whole 2x2x4 slice. The times are simulated.
32 devices in a mesh: batch: 2 (over y), gx: 4 (over z), gy: 4 (over x, core).
Axes of the slice: x: 2, y: 2, z: 4, core: 2. Of those that a mesh axis runs over, the one named last changes fastest.
Arguments:
- tokens: bfloat16 [64, 2, 18432], P(None, None, ('batch', 'gy')), may hold values from -6 to 6
- w_query: bfloat16 [18432, 12288], P(('batch', 'gy'), 'gx'), may hold values from -0.046875 to 0.046875
- w_keyval: bfloat16 [18432, 512], P(('batch', 'gy'), 'gx'), may hold values from -0.09375 to 0.09375
- w_out: bfloat16 [12288, 18432], P('gx', ('batch', 'gy')), may hold values from -0.19921875 to 0.19921875
- cache_keys: bfloat16 [64, 2048, 256], P(('batch', 'gx', 'gy')), may hold values from -140 to 140
- cache_values: bfloat16 [64, 2048, 256], P(('batch', 'gx', 'gy')), may hold values from -6 to 6
- lengths: int32 [64], P(('batch', 'gx', 'gy')), may hold values from 512 to 2048, as said below
Outputs:
- mixed: bfloat16 [64, 2, 18432], P('gx', None, ('batch', 'gy'))
Inputs may be any that keep to these rules, and one draw needn't show every extreme that they name: `lengths`: every draw has a sequence with 2048 valid positions and one with 512.
All inputs are finite; a program needn't handle non-finite values.
Results may differ from a plain program's by a relative error of at most 0.02.
Values may be sent and summed in bfloat16 or wider, within the bound.
No kernel may reach another device: no remote copies, remote signals or barrier semaphores. Data moves between devices by JAX's collectives and lax.ppermute only.
A program may use at most 128 MiB of HBM per device.

v0:
```python
import functools

import jax
import jax.numpy as jnp
import numpy as np
from jax import lax
from jax.experimental import pallas as pl
from jax.experimental.pallas import tpu as pltpu
from jax.sharding import Mesh
from jax.sharding import PartitionSpec as P

PLANE = ("batch", "gh", "gl")


def swapped_with(value, axes, sizes, differs):
    pairs = []
    for place in np.ndindex(*sizes):
        target = tuple(p ^ d for p, d in zip(place, differs))
        pairs.append((int(np.ravel_multi_index(place, sizes)), int(np.ravel_multi_index(target, sizes))))
    return lax.ppermute(value, axes, pairs)


def unxored(blocks, here):
    count = len(blocks)
    bit = 1
    while bit < count:
        turn = (here & bit) != 0
        blocks = [jnp.where(turn, blocks[k ^ bit], blocks[k]) for k in range(count)]
        bit *= 2
    return blocks


def farther_first(count):
    return [0, *range(2, count), 1]


def project_kernel(
    dims, blocks, chunks, tokens_hbm, query_hbm, pair_hbm, kept_out, given_out,
    tokens_ref, rows_ref, query_ref, pair_ref, kept_ref, given_ref, sum_ref, sems, out_sems,
):
    batch_count, gx_count, high_count, owned = dims
    query_cols = query_ref.shape[1]
    copies = [
        pltpu.make_async_copy(tokens_hbm, tokens_ref, sems.at[0]),
        pltpu.make_async_copy(pair_hbm, pair_ref, sems.at[1]),
    ]
    for place, (start, size) in enumerate(blocks):
        window = pl.ds(start, size)
        copies.append(pltpu.make_async_copy(query_hbm.at[window], query_ref.at[window], sems.at[place + 2]))
    for copy in copies:
        copy.start()
    steps, width = tokens_ref.shape[1:]
    block = gx_count * owned * steps
    half = rows_ref.shape[0] // 2
    copies[0].wait()
    for relative in range(2):
        low = lax.axis_index("gl") ^ relative
        for b in range(batch_count):
            for h in range(high_count):
                parts = []
                for g in range(gx_count):
                    first = (((b * gx_count + g) * high_count + h) * 2 + low) * owned
                    parts.append(tokens_ref[pl.ds(first, owned)])
                joined = jnp.concatenate(parts, axis=0).reshape(block, width)
                at = ((relative * batch_count + b) * high_count + h) * block
                rows_ref[pl.ds(at, block)] = joined
    writes = []

    def emit(product, start):
        product = product.astype(jnp.bfloat16)
        window = pl.ds(start, product.shape[1])
        kept_ref[:, window] = product[:half]
        given_ref[:, window] = product[half:]
        for source, target in ((given_ref, given_out), (kept_ref, kept_out)):
            copy = pltpu.make_async_copy(source.at[:, window], target.at[:, window], out_sems.at[len(writes)])
            copy.start()
            writes.append(copy)

    copies[1].wait()
    emit(jnp.dot(rows_ref[...], pair_ref[...], preferred_element_type=jnp.float32), query_cols)
    for place, (depth_at, depth) in enumerate(blocks):
        copies[2 + place].wait()
        rows = rows_ref[:, pl.ds(depth_at, depth)]
        for start, size in chunks:
            window = pl.ds(start, size)
            term = jnp.dot(
                rows, query_ref[pl.ds(depth_at, depth), window], preferred_element_type=jnp.float32
            )
            if place > 0:
                term = term + sum_ref[:, window]
            if place < len(blocks) - 1:
                sum_ref[:, window] = term
            else:
                emit(term, start)
    for copy in writes:
        copy.wait()


def cut(total, sizes):
    windows, start = [], 0
    while start < total:
        size = min(sizes[min(len(windows), len(sizes) - 1)], total - start)
        windows.append((start, size))
        start += size
    return windows


def project(tokens, w_query, w_keyval, dims):
    sequences, steps, width = tokens.shape
    query_cols, pair_cols = w_query.shape[1], w_keyval.shape[1]
    rows = sequences * steps
    blocks = cut(width, (768, 768, 512, 256))
    chunks = cut(query_cols, (768,))
    hbm = pl.BlockSpec(memory_space=pltpu.HBM)
    shape = jax.ShapeDtypeStruct((rows // 2, query_cols + pair_cols), jnp.bfloat16)
    return pl.pallas_call(
        functools.partial(project_kernel, dims, blocks, chunks),
        out_shape=(shape, shape),
        in_specs=[hbm, hbm, hbm],
        out_specs=(hbm, hbm),
        scratch_shapes=[
            pltpu.VMEM(tokens.shape, jnp.bfloat16),
            pltpu.VMEM((rows, width), jnp.bfloat16),
            pltpu.VMEM((width, query_cols), jnp.bfloat16),
            pltpu.VMEM((width, pair_cols), jnp.bfloat16),
            pltpu.VMEM((rows // 2, query_cols + pair_cols), jnp.bfloat16),
            pltpu.VMEM((rows // 2, query_cols + pair_cols), jnp.bfloat16),
            pltpu.VMEM((rows, query_cols), jnp.float32),
            pltpu.SemaphoreType.DMA((2 + len(blocks),)),
            pltpu.SemaphoreType.DMA((2 * (1 + len(chunks)),)),
        ],
        compiler_params=pltpu.CompilerParams(vmem_limit_bytes=62 * 1024 * 1024),
        cost_estimate=pl.CostEstimate(
            flops=2 * rows * width * (query_cols + pair_cols),
            bytes_accessed=2 * width * (query_cols + pair_cols),
            transcendentals=0,
        ),
        name="project",
    )(tokens, w_query, w_keyval)


def near_kernel(after_ref, source_ref, target_ref, token_ref, sem):
    copy = pltpu.make_async_copy(source_ref, target_ref, sem)
    copy.start()
    copy.wait()
    token_ref[...] = jnp.zeros_like(token_ref)


def near(after, array):
    anywhere = pl.BlockSpec(memory_space=pl.ANY)
    return pl.pallas_call(
        near_kernel,
        out_shape=(
            jax.ShapeDtypeStruct(array.shape, array.dtype),
            jax.ShapeDtypeStruct((8, 128), jnp.float32),
        ),
        in_specs=[anywhere, anywhere],
        out_specs=(anywhere, pl.BlockSpec(memory_space=pltpu.VMEM)),
        scratch_shapes=[pltpu.SemaphoreType.DMA],
        compiler_params=pltpu.CompilerParams(vmem_limit_bytes=36 * 1024 * 1024),
        cost_estimate=pl.CostEstimate(
            flops=0, bytes_accessed=2 * array.size * array.dtype.itemsize, transcendentals=0
        ),
        name="near",
    )(after, array)


def staged_kernel(source_ref, target_ref):
    target_ref[...] = source_ref[...]


def staged(array):
    vmem = pl.BlockSpec(memory_space=pltpu.VMEM)
    return pl.pallas_call(
        staged_kernel,
        out_shape=jax.ShapeDtypeStruct(array.shape, array.dtype),
        in_specs=[vmem],
        out_specs=vmem,
        compiler_params=pltpu.CompilerParams(vmem_limit_bytes=8 * 1024 * 1024),
        name="staged",
    )(array)


def combine_kernel(dims, kept_ref, taken_ref, own_ref, *sends):
    batch_count, high_count, block = dims
    for db in range(batch_count):
        for dh in range(high_count):
            at = ((lax.axis_index("batch") ^ db) * high_count + (lax.axis_index("gh") ^ dh)) * block
            window = pl.ds(pl.multiple_of(at, block), block)
            total = kept_ref[window].astype(jnp.float32) + taken_ref[window].astype(jnp.float32)
            target = sends[db * high_count + dh - 1] if db or dh else own_ref
            target[...] = total.astype(target.dtype)


def combine(kept, taken, dims):
    batch_count, high_count, block = dims
    cols = kept.shape[1]
    vmem = pl.BlockSpec(memory_space=pltpu.VMEM)
    count = batch_count * high_count
    return pl.pallas_call(
        functools.partial(combine_kernel, dims),
        out_shape=[jax.ShapeDtypeStruct((block, cols), jnp.float32)]
        + [jax.ShapeDtypeStruct((block, cols), jnp.bfloat16)] * (count - 1),
        in_specs=[vmem, vmem],
        out_specs=[vmem] * count,
        compiler_params=pltpu.CompilerParams(vmem_limit_bytes=8 * 1024 * 1024),
        name="combine",
    )(kept, taken)


def collect_kernel(count, own_ref, after_ref, *refs):
    received, outs, total_ref = refs[: -count - 1], refs[-count - 1 : -1], refs[-1]
    total = own_ref[...]
    for other in received:
        total = total + other[...].astype(jnp.float32)
    rows = outs[0].shape[0]
    for g in range(count):
        total_ref[g] = total[g * rows : (g + 1) * rows]
    for k in range(count):
        outs[k][...] = total_ref[lax.axis_index("gx") ^ k].astype(jnp.bfloat16)


def collect(own, received, after, gx_count):
    block, cols = own.shape
    rows = block // gx_count
    vmem = pl.BlockSpec(memory_space=pltpu.VMEM)
    return pl.pallas_call(
        functools.partial(collect_kernel, gx_count),
        out_shape=[jax.ShapeDtypeStruct((rows, cols), jnp.bfloat16)] * gx_count,
        in_specs=[vmem, pl.BlockSpec(memory_space=pl.ANY)]
        + [vmem] * len(received),
        out_specs=[vmem] * gx_count,
        scratch_shapes=[pltpu.VMEM((gx_count, rows, cols), jnp.float32)],
        compiler_params=pltpu.CompilerParams(vmem_limit_bytes=8 * 1024 * 1024),
        name="collect",
    )(own, after, *received)


def attend_kernel(dims, mask_ref, cos_ref, sin_ref, keys_ref, values_ref, *refs):
    gx_count, owned, steps, heads, width = dims
    blocks, outs = [None] * gx_count, refs[gx_count:-2]
    for k, ref in zip(farther_first(gx_count), refs):
        blocks[k] = ref
    rows_ref, result_ref = refs[-2:]
    query_cols = heads * width
    half = width // 2
    scaling = 1.0 / width**0.5
    count = gx_count * heads * steps
    cosine = jnp.concatenate([cos_ref[s] for s in range(owned)], axis=0)
    sine = jnp.concatenate([sin_ref[s] for s in range(owned)], axis=0)

    def turn(first, second, cosine, sine):
        return first * cosine - second * sine, second * cosine + first * sine

    scaled = (cosine * scaling, sine * scaling)

    key_value = [ref[:, pl.ds(query_cols, ref.shape[1] - query_cols)].astype(jnp.float32) for ref in blocks]
    key_value = jnp.concatenate(unxored(key_value, lax.axis_index("gx")), axis=1)
    new_values = key_value[:, width:]
    new_keys = turn(key_value[:, :half], key_value[:, half:width], cosine, sine)
    new_keys = jnp.concatenate(new_keys, axis=1).astype(jnp.bfloat16).astype(jnp.float32)
    for k in range(gx_count):
        for h in range(heads):
            first = blocks[k][:, pl.ds(h * width, half)].astype(jnp.float32)
            second = blocks[k][:, pl.ds(h * width + half, half)].astype(jnp.float32)
            for part, value in enumerate(turn(first, second, *scaled)):
                for s in range(owned):
                    window = pl.ds((k * heads + h) * steps, steps)
                    rows_ref[s, window, pl.ds(part * half, half)] = value[s * steps : (s + 1) * steps]
    step_of = lax.broadcasted_iota(jnp.int32, (count, 1), 0) % steps
    for s in range(owned):
        queries = rows_ref[s].astype(jnp.bfloat16)
        cached = lax.dot_general(
            queries, keys_ref[s], (((1,), (1,)), ((), ())), preferred_element_type=jnp.float32
        )
        cached = cached + mask_ref[s]
        highest = cached.max(-1, keepdims=True)
        wide = queries.astype(jnp.float32)
        fresh = []
        for u in range(steps):
            row = s * steps + u
            score = (wide * new_keys[row : row + 1]).sum(-1, keepdims=True)
            fresh.append(jnp.where(step_of >= u, score, -1e30))
            highest = jnp.maximum(highest, fresh[-1])
        exp_cached = jnp.exp(cached - highest)
        denom = exp_cached.sum(-1, keepdims=True)
        total = jnp.dot(
            exp_cached.astype(jnp.bfloat16), values_ref[s], preferred_element_type=jnp.float32
        )
        for u in range(steps):
            row = s * steps + u
            exp_fresh = jnp.exp(fresh[u] - highest)
            denom = denom + exp_fresh
            total = total + exp_fresh * new_values[row : row + 1]
        result_ref[s] = total * (1.0 / denom)
    for k in range(gx_count):
        for h in range(heads):
            window = pl.ds((k * heads + h) * steps, steps)
            value = jnp.concatenate([result_ref[s, window] for s in range(owned)], axis=0)
            outs[k][:, pl.ds(h * width, width)] = value.astype(jnp.bfloat16)


def attend(blocks, cache_keys, cache_values, lengths, query_cols):
    gx_count = len(blocks)
    owned, slots, width = cache_keys.shape
    rows = blocks[0].shape[0]
    steps = rows // owned
    heads = query_cols // width
    count = gx_count * heads * steps
    freqs = 10000.0 ** (-(jnp.arange(width // 2, dtype=jnp.float32) * 2.0 / width))
    positions = lengths[:, None, None] + jnp.arange(steps, dtype=jnp.int32)[None, :, None]
    angles = positions.astype(jnp.float32) * freqs
    mask = jnp.where(jnp.arange(slots)[None, None, :] < lengths[:, None, None], 0.0, -1e30)
    vmem = pl.BlockSpec(memory_space=pltpu.VMEM)
    return pl.pallas_call(
        functools.partial(attend_kernel, (gx_count, owned, steps, heads, width)),
        out_shape=[jax.ShapeDtypeStruct((rows, query_cols), jnp.bfloat16)] * gx_count,
        in_specs=[vmem] * (5 + gx_count),
        out_specs=[vmem] * gx_count,
        scratch_shapes=[
            pltpu.VMEM((owned, count, width), jnp.float32),
            pltpu.VMEM((owned, count, width), jnp.float32),
        ],
        compiler_params=pltpu.CompilerParams(vmem_limit_bytes=12 * 1024 * 1024),
        cost_estimate=pl.CostEstimate(
            flops=4 * owned * count * slots * width,
            bytes_accessed=4 * owned * slots * width,
            transcendentals=owned * count * slots,
        ),
        name="attend",
    )(mask, jnp.cos(angles), jnp.sin(angles), cache_keys, cache_values, *[blocks[k] for k in farther_first(gx_count)])


def order_kernel(distances, *refs):
    out_ref, sorted_ref = refs[-2:]
    for k, block in zip(distances, refs):
        sorted_ref[lax.axis_index("gx") ^ k] = block[...].astype(jnp.float32)
    parts = [sorted_ref[g] for g in range(len(distances))]
    out_ref[...] = jnp.concatenate(parts, axis=0).astype(out_ref.dtype)


def order(blocks):
    vmem = pl.BlockSpec(memory_space=pltpu.VMEM)
    rows, cols = blocks[0].shape
    count = len(blocks)
    distances = farther_first(count)
    return pl.pallas_call(
        functools.partial(order_kernel, distances),
        out_shape=jax.ShapeDtypeStruct((count * rows, cols), blocks[0].dtype),
        in_specs=[vmem] * count,
        out_specs=vmem,
        scratch_shapes=[pltpu.VMEM((count, rows, cols), jnp.float32)],
        compiler_params=pltpu.CompilerParams(vmem_limit_bytes=8 * 1024 * 1024),
        name="order",
    )(*[blocks[k] for k in distances])


def mix_kernel(dims, chunk, part, weight_ref, *refs):
    batch_count, gx_count, high_count, block = dims
    count = 2 * batch_count * high_count
    blocks, own_ref, sends, (rows_ref, sum_ref) = refs[:count][::-1], refs[count], refs[count + 1 : -2], refs[-2:]
    shards = gx_count // batch_count
    group = block // shards
    for relative in range(2):
        for db in range(batch_count):
            for dh in range(high_count):
                b, h = lax.axis_index("batch") ^ db, lax.axis_index("gh") ^ dh
                at = ((relative * batch_count + b) * high_count + h) * block
                source = blocks[(relative * batch_count + db) * high_count + dh]
                rows_ref[pl.ds(pl.multiple_of(at, block), block)] = source[...]
    lhs = rows_ref[...]
    first, out_cols = part
    for start in range(0, out_cols, chunk):
        size = min(chunk, out_cols - start)
        window = pl.ds(start, size)
        sum_ref[:, pl.ds(0, size)] = jnp.dot(
            lhs, weight_ref[:, pl.ds(first + start, size)], preferred_element_type=jnp.float32
        )
        for k in range(gx_count):
            shard = lax.axis_index("gx") ^ k
            b, hi = shard // shards, shard % shards
            parts = []
            for relative in range(2):
                for h in range(high_count):
                    at = ((relative * batch_count + b) * high_count + h) * block + hi * group
                    at = pl.multiple_of(at, group)
                    parts.append(sum_ref[pl.ds(at, group), pl.ds(0, size)])
            piece = jnp.concatenate(parts, axis=0)
            target = own_ref if k == 0 else sends[k - 1]
            target[:, window] = piece.astype(target.dtype)


def mix(blocks, w_out, dims, part):
    batch_count, gx_count, high_count, block = dims
    depth = w_out.shape[0]
    out_cols = part[1]
    rows = len(blocks) * block
    chunk = min(768, out_cols)
    vmem = pl.BlockSpec(memory_space=pltpu.VMEM)
    kept = (0, 2) if gx_count == 4 else (0,)
    shapes = [
        jax.ShapeDtypeStruct((rows // gx_count, out_cols), jnp.float32 if k in kept else jnp.bfloat16)
        for k in range(gx_count)
    ]
    return pl.pallas_call(
        functools.partial(mix_kernel, dims, chunk, part),
        out_shape=shapes,
        in_specs=[vmem] * (1 + len(blocks)),
        out_specs=[vmem] * gx_count,
        scratch_shapes=[pltpu.VMEM((rows, depth), jnp.bfloat16), pltpu.VMEM((rows, chunk), jnp.float32)],
        compiler_params=pltpu.CompilerParams(vmem_limit_bytes=20 * 1024 * 1024),
        cost_estimate=pl.CostEstimate(
            flops=2 * rows * depth * out_cols, bytes_accessed=2 * depth * out_cols, transcendentals=0
        ),
        name="mix",
    )(w_out, *blocks[::-1])


def relay_kernel(own_ref, taken_ref, near_ref, sum_ref, copy_ref):
    total = own_ref[...] + taken_ref[...].astype(jnp.float32)
    sum_ref[...] = total.astype(sum_ref.dtype)
    copy_ref[...] = near_ref[...]


def relay(own, taken, near):
    vmem = pl.BlockSpec(memory_space=pltpu.VMEM)
    return pl.pallas_call(
        relay_kernel,
        out_shape=[jax.ShapeDtypeStruct(near.shape, near.dtype)] * 2,
        in_specs=[vmem] * 3,
        out_specs=[vmem] * 2,
        compiler_params=pltpu.CompilerParams(vmem_limit_bytes=8 * 1024 * 1024),
        name="relay",
    )(own, taken, near)


def summed_terms(sends):
    count = len(sends) + 1
    if count != 4:
        return [swapped_with(sends[k - 1], "gx", (count,), (k,)) for k in farther_first(count)[1:]]
    near, far, farthest = sends
    taken = swapped_with(farthest, "gx", (count,), (1,))
    both, near = relay(far, taken, near)
    return [swapped_with(both, "gx", (count,), (2,)), swapped_with(near, "gx", (count,), (1,))]


def finish_kernel(dims, own_ref, *refs):
    received, out_ref = refs[: len(refs) - 1], refs[-1]
    batch_count, high_count, owned = dims
    steps, out_cols = out_ref.shape[1:]
    size = batch_count * owned * steps
    received = [ref for ref in received if ref.shape == own_ref.shape]
    for relative in range(2):
        low = lax.axis_index("gl") ^ relative
        for h in range(high_count):
            window = pl.ds((relative * high_count + h) * size, size)
            total = own_ref[window]
            for other in received:
                total = total + other[window].astype(jnp.float32)
            total = total.reshape(batch_count, owned, steps, out_cols).astype(jnp.bfloat16)
            for g in range(batch_count):
                first = ((g * high_count + h) * 2 + low) * owned
                out_ref[pl.ds(first, owned)] = total[g]


def finish(own, received, dims, steps, part, parts, before):
    rows, out_cols = own.shape
    whole = pl.BlockSpec((rows, out_cols), lambda step: (0, 0))
    operands = [own, *received]
    in_specs = [whole] * len(operands)
    aliases = {}
    if before is not None:
        aliases[len(operands)] = 0
        operands.append(before)
        in_specs.append(pl.BlockSpec(memory_space=pl.ANY))
    return pl.pallas_call(
        functools.partial(finish_kernel, dims),
        grid=(1,),
        out_shape=jax.ShapeDtypeStruct((rows // steps, steps, out_cols * parts), jnp.bfloat16),
        in_specs=in_specs,
        out_specs=pl.BlockSpec((rows // steps, steps, out_cols), lambda step: (0, 0, part)),
        input_output_aliases=aliases,
        compiler_params=pltpu.CompilerParams(vmem_limit_bytes=16 * 1024 * 1024),
        name="finish",
    )(*operands)


def local(tokens, w_query, w_keyval, w_out, cache_keys, cache_values, lengths):
    batch_count = lax.axis_size("batch")
    gx_count = lax.axis_size("gx")
    high_count = lax.axis_size("gh")
    sizes = (batch_count, high_count, 2)
    owned = cache_keys.shape[0]
    sequences, steps, width = tokens.shape
    query_cols = w_query.shape[1]
    rows = owned * steps
    rows_here = gx_count * rows

    kept, given = project(tokens, w_query, w_keyval, (batch_count, gx_count, high_count, owned))
    taken = swapped_with(given, PLANE, sizes, (0, 0, 1))
    far = [(db, dh) for db in range(batch_count) for dh in range(high_count)][1:]
    own, *sends = combine(staged(kept), taken, (batch_count, high_count, rows_here))
    received = [
        swapped_with(block, PLANE, sizes, (db, dh, 0)) for block, (db, dh) in zip(sends, far)
    ]
    w_out, token = near(own, w_out)
    blocks = collect(own, received, token, gx_count)
    blocks = [blocks[0]] + [
        swapped_with(blocks[k], "gx", (gx_count,), (k,)) for k in range(1, gx_count)
    ]
    blocks = attend(blocks, cache_keys, cache_values, lengths, query_cols)
    blocks = [blocks[0]] + [
        swapped_with(blocks[k], "gx", (gx_count,), (k,)) for k in range(1, gx_count)
    ]
    grouped = order(blocks)

    ours = [grouped] + [swapped_with(grouped, PLANE, sizes, (db, dh, 0)) for db, dh in far]
    theirs = [swapped_with(block, PLANE, sizes, (0, 0, 1)) for block in ours]
    out_cols = w_out.shape[1]
    parts = 2 if out_cols % 256 == 0 else 1
    size = out_cols // parts
    mixed = None
    products = [
        mix(ours + theirs, w_out, (batch_count, gx_count, high_count, rows_here), (part * size, size))
        for part in range(parts)
    ]
    for part, (own, *sends) in enumerate(products):
        received = summed_terms(sends)
        mixed = finish(own, received, (batch_count, high_count, owned), steps, part, parts, mixed)
    return mixed


def solution(mesh):
    batch_count, gx_count, gy_count = mesh.devices.shape
    split = Mesh(
        mesh.devices.reshape(batch_count, gx_count, gy_count // 2, 2), ("batch", "gx", "gh", "gl")
    )
    plane = ("batch", "gh", "gl")
    placed = (
        P(None, None, plane),
        P(plane, "gx"),
        P(plane, "gx"),
        P("gx", plane),
        P(("batch", "gx", "gh", "gl"), None, None),
        P(("batch", "gx", "gh", "gl"), None, None),
        P(("batch", "gx", "gh", "gl")),
    )
    return jax.shard_map(
        local, mesh=split, in_specs=placed, out_specs=P("gx", None, plane), check_vma=False
    )
```

profile of v0, /device:TPU:0, one launch (start us, length us, event | category | flops | bytes accessed | tf_op | source)
XLA Modules:
  0.0 61.2 jit_solution(457215862964642712)
XLA Ops:
  0.0 6.8 %project.1 = (bf16[64,3200]{1,0:T(8,128)(2,1)}, bf16[64,3200]{1,0:T(8,128)(2,1)}) custom-call(bf16[64,2,2304]{2,1,0:T(2,128)(2,1)} %tokens_hbm.1, bf16[2304,3072]{1,0:T(8,128)(2,1)} %query_hbm.1, bf16[2304,128]{1,0:T(8,128)(2,1)} %pair_hbm.1), custom_call_target="tpu_custom_call" | custom-call | flops 1887436800 | bytes 14745600 | tf_op jit(solution)/shard_map/project/pallas_call | solution.py:116
  7.3 1.3 %copy-done.2 = bf16[64,3200]{1,0:T(8,128)(2,1)S(1)} copy-done((bf16[64,3200]{1,0:T(8,128)(2,1)S(1)}, bf16[64,3200]{1,0:T(8,128)(2,1)}, u32[]{:S(2)}) %copy-start.2) | copy-done | bytes 409624
  9.0 2.9 %collective-permute-start.1 = (bf16[16,3200]{1,0:T(8,128)(2,1)S(1)}, bf16[16,3200]{1,0:T(8,128)(2,1)S(1)}, u32[]{:S(2)}, u32[]{:S(2)}) collective-permute-start(bf16[16,3200]{1,0:T(8,128)(2,1)S(1)} %get-tuple-element.38), channel_id=1, source_target_pairs={{0,2},{1,3},{2,0},{3,1},{16,18},{17,19},{18,16},{19,17},{4,6},{5,7... | collective-permute-start | bytes 307208 | tf_op jit(solution)/shard_map/ppermute | solution.py:20
  11.9 1.5 %collective-permute-start.2 = (bf16[16,3200]{1,0:T(8,128)(2,1)S(1)}, bf16[16,3200]{1,0:T(8,128)(2,1)S(1)}, u32[]{:S(2)}, u32[]{:S(2)}) collective-permute-start(bf16[16,3200]{1,0:T(8,128)(2,1)S(1)} %get-tuple-element.39), channel_id=1, source_target_pairs={{0,16},{1,17},{2,18},{3,19},{16,0},{17,1},{18,2},{19,3},{4,20},{5,... | collective-permute-start | bytes 307208 | tf_op jit(solution)/shard_map/ppermute | solution.py:20
  13.5 5.0 %near.1 = (bf16[3072,2304]{1,0:T(8,128)(2,1)S(1)}, f32[8,128]{1,0:T(8,128)S(1)}) custom-call(f32[16,3200]{1,0:T(8,128)S(1)} %get-tuple-element.35.after_ref.own_ref, bf16[3072,2304]{1,0:T(8,128)(2,1)} %source_ref.1), custom_call_target="tpu_custom_call" | custom-call | bytes 28311552 | tf_op jit(solution)/shard_map/near/pallas_call | solution.py:151
  19.1 2.7 %collective-permute-start.4 = (bf16[4,3200]{1,0:T(4,128)(2,1)S(1)}, bf16[4,3200]{1,0:T(4,128)(2,1)S(1)}, u32[]{:S(2)}, u32[]{:S(2)}) collective-permute-start(bf16[4,3200]{1,0:T(4,128)(2,1)S(1)} %get-tuple-element.42), channel_id=1, source_target_pairs={{0,8},{4,12},{8,0},{12,4},{1,9},{5,13},{9,1},{13,5},{2,10},{6,14},... | collective-permute-start | bytes 76808 | tf_op jit(solution)/shard_map/ppermute | solution.py:20
  21.8 1.4 %collective-permute-start.5 = (bf16[4,3200]{1,0:T(4,128)(2,1)S(1)}, bf16[4,3200]{1,0:T(4,128)(2,1)S(1)}, u32[]{:S(2)}, u32[]{:S(2)}) collective-permute-start(bf16[4,3200]{1,0:T(4,128)(2,1)S(1)} %get-tuple-element.43), channel_id=1, source_target_pairs={{0,12},{4,8},{8,4},{12,0},{1,13},{5,9},{9,5},{13,1},{2,14},{6,10},... | collective-permute-start | bytes 76808 | tf_op jit(solution)/shard_map/ppermute | solution.py:20
  23.9 3.5 %collective-permute-done.5.refs_2_ = bf16[4,3200]{1,0:T(4,128)(2,1)S(1)} collective-permute-done((bf16[4,3200]{1,0:T(4,128)(2,1)S(1)}, bf16[4,3200]{1,0:T(4,128)(2,1)S(1)}, u32[]{:S(2)}, u32[]{:S(2)}) %collective-permute-start.5) | collective-permute-done | bytes 25632 | tf_op jit(solution)/shard_map/ppermute | solution.py:20
  27.4 1.8 %attend.1 = (bf16[4,3072]{1,0:T(4,128)(2,1)S(1)}, bf16[4,3072]{1,0:T(4,128)(2,1)S(1)}, bf16[4,3072]{1,0:T(4,128)(2,1)S(1)}, bf16[4,3072]{1,0:T(4,128)(2,1)S(1)}) custom-call(f32[2,1,2048]{2,1,0:T(1,128)S(1)} %compare_select_fusion.mask_ref, f32[2,2,128]{2,1,0:T(2,128)S(1)} %get-tuple-element.62.cos_ref, f32[2,2,128]{2,1,0:T(2,128)S(1)} %get-tuple-element.61.sin_ref, ...), custom_call_target="tpu_custom_call" | custom-call | flops 402653184 | bytes 4194304 | tf_op jit(solution)/shard_map/attend/pallas_call | solution.py:315
  29.2 1.3 %collective-permute-start.7 = (bf16[4,3072]{1,0:T(4,128)(2,1)S(1)}, bf16[4,3072]{1,0:T(4,128)(2,1)S(1)}, u32[]{:S(2)}, u32[]{:S(2)}) collective-permute-start(bf16[4,3072]{1,0:T(4,128)(2,1)S(1)} %get-tuple-element.46), channel_id=1, source_target_pairs={{0,8},{4,12},{8,0},{12,4},{1,9},{5,13},{9,1},{13,5},{2,10},{6,14},... | collective-permute-start | bytes 73736 | tf_op jit(solution)/shard_map/ppermute | solution.py:20
  31.5 1.3 %collective-permute-start.9 = (bf16[4,3072]{1,0:T(4,128)(2,1)S(1)}, bf16[4,3072]{1,0:T(4,128)(2,1)S(1)}, u32[]{:S(2)}, u32[]{:S(2)}) collective-permute-start(bf16[4,3072]{1,0:T(4,128)(2,1)S(1)} %get-tuple-element.48), channel_id=1, source_target_pairs={{0,4},{4,0},{8,12},{12,8},{1,5},{5,1},{9,13},{13,9},{2,6},{6,2},{1... | collective-permute-start | bytes 73736 | tf_op jit(solution)/shard_map/ppermute | solution.py:20
  32.8 1.2 %collective-permute-done.7.refs_1_ = bf16[4,3072]{1,0:T(4,128)(2,1)S(1)} collective-permute-done((bf16[4,3072]{1,0:T(4,128)(2,1)S(1)}, bf16[4,3072]{1,0:T(4,128)(2,1)S(1)}, u32[]{:S(2)}, u32[]{:S(2)}) %collective-permute-start.7) | collective-permute-done | bytes 24608 | tf_op jit(solution)/shard_map/ppermute | solution.py:20
  34.0 2.1 %collective-permute-done.8.refs_2_ = bf16[4,3072]{1,0:T(4,128)(2,1)S(1)} collective-permute-done((bf16[4,3072]{1,0:T(4,128)(2,1)S(1)}, bf16[4,3072]{1,0:T(4,128)(2,1)S(1)}, u32[]{:S(2)}, u32[]{:S(2)}) %collective-permute-start.8) | collective-permute-done | bytes 24608 | tf_op jit(solution)/shard_map/ppermute | solution.py:20
  36.2 2.5 %collective-permute-start.10 = (bf16[16,3072]{1,0:T(8,128)(2,1)S(1)}, bf16[16,3072]{1,0:T(8,128)(2,1)S(1)}, u32[]{:S(2)}, u32[]{:S(2)}) collective-permute-start(bf16[16,3072]{1,0:T(8,128)(2,1)S(1)} %order.1.refs_7_), channel_id=1, source_target_pairs={{0,18},{1,19},{2,16},{3,17},{16,2},{17,3},{18,0},{19,1},{4,22},{5,... | collective-permute-start | bytes 294920 | tf_op jit(solution)/shard_map/ppermute | solution.py:20
  39.8 2.0 %collective-permute-done.10.refs_4_ = bf16[16,3072]{1,0:T(8,128)(2,1)S(1)} collective-permute-done((bf16[16,3072]{1,0:T(8,128)(2,1)S(1)}, bf16[16,3072]{1,0:T(8,128)(2,1)S(1)}, u32[]{:S(2)}, u32[]{:S(2)}) %collective-permute-start.10) | collective-permute-done | bytes 98336 | tf_op jit(solution)/shard_map/ppermute | solution.py:20
  41.8 1.5 %collective-permute-done.12.refs_5_ = bf16[16,3072]{1,0:T(8,128)(2,1)S(1)} collective-permute-done((bf16[16,3072]{1,0:T(8,128)(2,1)S(1)}, bf16[16,3072]{1,0:T(8,128)(2,1)S(1)}, u32[]{:S(2)}, u32[]{:S(2)}) %collective-permute-start.12) | collective-permute-done | bytes 98336 | tf_op jit(solution)/shard_map/ppermute | solution.py:20
  45.2 1.3 %mix.3 = (f32[32,1152]{1,0:T(8,128)S(1)}, bf16[32,1152]{1,0:T(8,128)(2,1)S(1)}, f32[32,1152]{1,0:T(8,128)S(1)}, bf16[32,1152]{1,0:T(8,128)(2,1)S(1)}) custom-call(bf16[3072,2304]{1,0:T(8,128)(2,1)S(1)} %get-tuple-element.36.weight_ref, bf16[16,3072]{1,0:T(8,128)(2,1)S(1)} %collective-permute-done.11.refs_0_, ...), custom_call_target="tpu_custom_call" | custom-call | flops 905969664 | bytes 7077888 | tf_op jit(solution)/shard_map/mix/pallas_call | solution.py:405
  47.0 1.3 %mix.2 = (f32[32,1152]{1,0:T(8,128)S(1)}, bf16[32,1152]{1,0:T(8,128)(2,1)S(1)}, f32[32,1152]{1,0:T(8,128)S(1)}, bf16[32,1152]{1,0:T(8,128)(2,1)S(1)}) custom-call(bf16[3072,2304]{1,0:T(8,128)(2,1)S(1)} %get-tuple-element.36.weight_ref, bf16[16,3072]{1,0:T(8,128)(2,1)S(1)} %collective-permute-done.11.refs_0_, ...), custom_call_target="tpu_custom_call" | custom-call | flops 905969664 | bytes 7077888 | tf_op jit(solution)/shard_map/mix/pallas_call | solution.py:405
  48.3 1.6 %collective-permute-start.17 = (bf16[32,1152]{1,0:T(8,128)(2,1)S(1)}, bf16[32,1152]{1,0:T(8,128)(2,1)S(1)}, u32[]{:S(2)}, u32[]{:S(2)}) collective-permute-start(bf16[32,1152]{1,0:T(8,128)(2,1)S(1)} %get-tuple-element.51), channel_id=1, source_target_pairs={{0,4},{4,0},{8,12},{12,8},{1,5},{5,1},{9,13},{13,9},{2,6},{6,2},{1... | collective-permute-start | bytes 221192 | tf_op jit(solution)/shard_map/ppermute | solution.py:20
  50.0 1.0 %collective-permute-done.20.taken_ref = bf16[32,1152]{1,0:T(8,128)(2,1)S(1)} collective-permute-done((bf16[32,1152]{1,0:T(8,128)(2,1)S(1)}, bf16[32,1152]{1,0:T(8,128)(2,1)S(1)}, u32[]{:S(2)}, u32[]{:S(2)}) %collective-permute-start.20) | collective-permute-done | bytes 73760 | tf_op jit(solution)/shard_map/ppermute | solution.py:20
  51.0 1.0 %collective-permute-start.21 = (bf16[32,1152]{1,0:T(8,128)(2,1)S(1)}, bf16[32,1152]{1,0:T(8,128)(2,1)S(1)}, u32[]{:S(2)}, u32[]{:S(2)}) collective-permute-start(bf16[32,1152]{1,0:T(8,128)(2,1)S(1)} %get-tuple-element.59), channel_id=1, source_target_pairs={{0,8},{4,12},{8,0},{12,4},{1,9},{5,13},{9,1},{13,5},{2,10},{6,14},... | collective-permute-start | bytes 221192 | tf_op jit(solution)/shard_map/ppermute | solution.py:20
  52.0 1.7 %collective-permute-start.22 = (bf16[32,1152]{1,0:T(8,128)(2,1)S(1)}, bf16[32,1152]{1,0:T(8,128)(2,1)S(1)}, u32[]{:S(2)}, u32[]{:S(2)}) collective-permute-start(bf16[32,1152]{1,0:T(8,128)(2,1)S(1)} %get-tuple-element.60), channel_id=1, source_target_pairs={{0,4},{4,0},{8,12},{12,8},{1,5},{5,1},{9,13},{13,9},{2,6},{6,2},{1... | collective-permute-start | bytes 221192 | tf_op jit(solution)/shard_map/ppermute | solution.py:20
  53.7 2.1 %collective-permute-start.18 = (bf16[32,1152]{1,0:T(8,128)(2,1)S(1)}, bf16[32,1152]{1,0:T(8,128)(2,1)S(1)}, u32[]{:S(2)}, u32[]{:S(2)}) collective-permute-start(bf16[32,1152]{1,0:T(8,128)(2,1)S(1)} %get-tuple-element.53), channel_id=1, source_target_pairs={{0,8},{4,12},{8,0},{12,4},{1,9},{5,13},{9,1},{13,5},{2,10},{6,14},... | collective-permute-start | bytes 221192 | tf_op jit(solution)/shard_map/ppermute | solution.py:20
  56.1 2.5 %collective-permute-done.21.refs_0_ = bf16[32,1152]{1,0:T(8,128)(2,1)S(1)} collective-permute-done((bf16[32,1152]{1,0:T(8,128)(2,1)S(1)}, bf16[32,1152]{1,0:T(8,128)(2,1)S(1)}, u32[]{:S(2)}, u32[]{:S(2)}) %collective-permute-start.21) | collective-permute-done | bytes 73760 | tf_op jit(solution)/shard_map/ppermute | solution.py:20
  (47 shorter events, 9.6 us)
Async XLA Ops:
  6.8 20.6 %copy-start = (bf16[2,2048,256]{2,1,0:T(8,128)(2,1)S(1)}, bf16[2,2048,256]{2,1,0:T(8,128)(2,1)}, u32[]{:S(2)}) copy-start(bf16[2,2048,256]{2,1,0:T(8,128)(2,1)} %keys_ref.1) | copy-start | bytes 6291460
  6.8 2.1 %collective-permute-start = (bf16[64,3200]{1,0:T(8,128)(2,1)}, bf16[64,3200]{1,0:T(8,128)(2,1)S(1)}, u32[]{:S(2)}, u32[]{:S(2)}) collective-permute-start(bf16[64,3200]{1,0:T(8,128)(2,1)} %get-tuple-element.34), channel_id=1, source_target_pairs={{0,1},{1,0},{2,3},{3,2},{16,17},{17,16},{18,19},{19,18},{4,5},{5,4... | collective-permute-start | bytes 1228808 | tf_op jit(solution)/shard_map/ppermute | solution.py:20
  9.0 9.5 %collective-permute-start.1 = (bf16[16,3200]{1,0:T(8,128)(2,1)S(1)}, bf16[16,3200]{1,0:T(8,128)(2,1)S(1)}, u32[]{:S(2)}, u32[]{:S(2)}) collective-permute-start(bf16[16,3200]{1,0:T(8,128)(2,1)S(1)} %get-tuple-element.38), channel_id=1, source_target_pairs={{0,2},{1,3},{2,0},{3,1},{16,18},{17,19},{18,16},{19,17},{4,6},{5,7... | collective-permute-start | bytes 307208 | tf_op jit(solution)/shard_map/ppermute | solution.py:20
  11.9 6.6 %collective-permute-start.2 = (bf16[16,3200]{1,0:T(8,128)(2,1)S(1)}, bf16[16,3200]{1,0:T(8,128)(2,1)S(1)}, u32[]{:S(2)}, u32[]{:S(2)}) collective-permute-start(bf16[16,3200]{1,0:T(8,128)(2,1)S(1)} %get-tuple-element.39), channel_id=1, source_target_pairs={{0,16},{1,17},{2,18},{3,19},{16,0},{17,1},{18,2},{19,3},{4,20},{5,... | collective-permute-start | bytes 307208 | tf_op jit(solution)/shard_map/ppermute | solution.py:20
  13.5 5.6 %collective-permute-start.3 = (bf16[16,3200]{1,0:T(8,128)(2,1)S(1)}, bf16[16,3200]{1,0:T(8,128)(2,1)S(1)}, u32[]{:S(2)}, u32[]{:S(2)}) collective-permute-start(bf16[16,3200]{1,0:T(8,128)(2,1)S(1)} %get-tuple-element.40), channel_id=1, source_target_pairs={{0,18},{1,19},{2,16},{3,17},{16,2},{17,3},{18,0},{19,1},{4,22},{5,... | collective-permute-start | bytes 307208 | tf_op jit(solution)/shard_map/ppermute | solution.py:20
  19.1 4.8 %collective-permute-start.4 = (bf16[4,3200]{1,0:T(4,128)(2,1)S(1)}, bf16[4,3200]{1,0:T(4,128)(2,1)S(1)}, u32[]{:S(2)}, u32[]{:S(2)}) collective-permute-start(bf16[4,3200]{1,0:T(4,128)(2,1)S(1)} %get-tuple-element.42), channel_id=1, source_target_pairs={{0,8},{4,12},{8,0},{12,4},{1,9},{5,13},{9,1},{13,5},{2,10},{6,14},... | collective-permute-start | bytes 76808 | tf_op jit(solution)/shard_map/ppermute | solution.py:20
  21.8 5.6 %collective-permute-start.5 = (bf16[4,3200]{1,0:T(4,128)(2,1)S(1)}, bf16[4,3200]{1,0:T(4,128)(2,1)S(1)}, u32[]{:S(2)}, u32[]{:S(2)}) collective-permute-start(bf16[4,3200]{1,0:T(4,128)(2,1)S(1)} %get-tuple-element.43), channel_id=1, source_target_pairs={{0,12},{4,8},{8,4},{12,0},{1,13},{5,9},{9,5},{13,1},{2,14},{6,10},... | collective-permute-start | bytes 76808 | tf_op jit(solution)/shard_map/ppermute | solution.py:20
  23.1 4.3 %collective-permute-start.6 = (bf16[4,3200]{1,0:T(4,128)(2,1)S(1)}, bf16[4,3200]{1,0:T(4,128)(2,1)S(1)}, u32[]{:S(2)}, u32[]{:S(2)}) collective-permute-start(bf16[4,3200]{1,0:T(4,128)(2,1)S(1)} %get-tuple-element.44), channel_id=1, source_target_pairs={{0,4},{4,0},{8,12},{12,8},{1,5},{5,1},{9,13},{13,9},{2,6},{6,2},{1... | collective-permute-start | bytes 76808 | tf_op jit(solution)/shard_map/ppermute | solution.py:20
  29.2 4.8 %collective-permute-start.7 = (bf16[4,3072]{1,0:T(4,128)(2,1)S(1)}, bf16[4,3072]{1,0:T(4,128)(2,1)S(1)}, u32[]{:S(2)}, u32[]{:S(2)}) collective-permute-start(bf16[4,3072]{1,0:T(4,128)(2,1)S(1)} %get-tuple-element.46), channel_id=1, source_target_pairs={{0,8},{4,12},{8,0},{12,4},{1,9},{5,13},{9,1},{13,5},{2,10},{6,14},... | collective-permute-start | bytes 73736 | tf_op jit(solution)/shard_map/ppermute | solution.py:20
  30.5 5.6 %collective-permute-start.8 = (bf16[4,3072]{1,0:T(4,128)(2,1)S(1)}, bf16[4,3072]{1,0:T(4,128)(2,1)S(1)}, u32[]{:S(2)}, u32[]{:S(2)}) collective-permute-start(bf16[4,3072]{1,0:T(4,128)(2,1)S(1)} %get-tuple-element.47), channel_id=1, source_target_pairs={{0,12},{4,8},{8,4},{12,0},{1,13},{5,9},{9,5},{13,1},{2,14},{6,10},... | collective-permute-start | bytes 73736 | tf_op jit(solution)/shard_map/ppermute | solution.py:20
  31.5 4.7 %collective-permute-start.9 = (bf16[4,3072]{1,0:T(4,128)(2,1)S(1)}, bf16[4,3072]{1,0:T(4,128)(2,1)S(1)}, u32[]{:S(2)}, u32[]{:S(2)}) collective-permute-start(bf16[4,3072]{1,0:T(4,128)(2,1)S(1)} %get-tuple-element.48), channel_id=1, source_target_pairs={{0,4},{4,0},{8,12},{12,8},{1,5},{5,1},{9,13},{13,9},{2,6},{6,2},{1... | collective-permute-start | bytes 73736 | tf_op jit(solution)/shard_map/ppermute | solution.py:20
  36.2 5.6 %collective-permute-start.10 = (bf16[16,3072]{1,0:T(8,128)(2,1)S(1)}, bf16[16,3072]{1,0:T(8,128)(2,1)S(1)}, u32[]{:S(2)}, u32[]{:S(2)}) collective-permute-start(bf16[16,3072]{1,0:T(8,128)(2,1)S(1)} %order.1.refs_7_), channel_id=1, source_target_pairs={{0,18},{1,19},{2,16},{3,17},{16,2},{17,3},{18,0},{19,1},{4,22},{5,... | collective-permute-start | bytes 294920 | tf_op jit(solution)/shard_map/ppermute | solution.py:20
  38.7 4.6 %collective-permute-start.12 = (bf16[16,3072]{1,0:T(8,128)(2,1)S(1)}, bf16[16,3072]{1,0:T(8,128)(2,1)S(1)}, u32[]{:S(2)}, u32[]{:S(2)}) collective-permute-start(bf16[16,3072]{1,0:T(8,128)(2,1)S(1)} %order.1.refs_7_), channel_id=1, source_target_pairs={{0,16},{1,17},{2,18},{3,19},{16,0},{17,1},{18,2},{19,3},{4,20},{5,... | collective-permute-start | bytes 294920 | tf_op jit(solution)/shard_map/ppermute | solution.py:20
  39.2 4.6 %collective-permute-start.14 = (bf16[16,3072]{1,0:T(8,128)(2,1)S(1)}, bf16[16,3072]{1,0:T(8,128)(2,1)S(1)}, u32[]{:S(2)}, u32[]{:S(2)}) collective-permute-start(bf16[16,3072]{1,0:T(8,128)(2,1)S(1)} %order.1.refs_7_), channel_id=1, source_target_pairs={{0,2},{1,3},{2,0},{3,1},{16,18},{17,19},{18,16},{19,17},{4,6},{5,7... | collective-permute-start | bytes 294920 | tf_op jit(solution)/shard_map/ppermute | solution.py:20
  39.8 4.1 %collective-permute-start.16 = (bf16[16,3072]{1,0:T(8,128)(2,1)S(1)}, bf16[16,3072]{1,0:T(8,128)(2,1)S(1)}, u32[]{:S(2)}, u32[]{:S(2)}) collective-permute-start(bf16[16,3072]{1,0:T(8,128)(2,1)S(1)} %order.1.refs_7_), channel_id=1, source_target_pairs={{0,1},{1,0},{2,3},{3,2},{16,17},{17,16},{18,19},{19,18},{4,5},{5,4... | collective-permute-start | bytes 294920 | tf_op jit(solution)/shard_map/ppermute | solution.py:20
  41.8 2.1 %collective-permute-start.11 = (bf16[16,3072]{1,0:T(8,128)(2,1)S(1)}, bf16[16,3072]{1,0:T(8,128)(2,1)S(1)}, u32[]{:S(2)}, u32[]{:S(2)}) collective-permute-start(bf16[16,3072]{1,0:T(8,128)(2,1)S(1)} %collective-permute-done.10.refs_4_), channel_id=1, source_target_pairs={{0,1},{1,0},{2,3},{3,2},{16,17},{17,16},{18,19},{19,18},{4,5},{5,4... | collective-permute-start | bytes 294920 | tf_op jit(solution)/shard_map/ppermute | solution.py:20
  43.4 1.3 %collective-permute-start.13 = (bf16[16,3072]{1,0:T(8,128)(2,1)S(1)}, bf16[16,3072]{1,0:T(8,128)(2,1)S(1)}, u32[]{:S(2)}, u32[]{:S(2)}) collective-permute-start(bf16[16,3072]{1,0:T(8,128)(2,1)S(1)} %collective-permute-done.12.refs_5_), channel_id=1, source_target_pairs={{0,1},{1,0},{2,3},{3,2},{16,17},{17,16},{18,19},{19,18},{4,5},{5,4... | collective-permute-start | bytes 294920 | tf_op jit(solution)/shard_map/ppermute | solution.py:20
  43.9 1.3 %collective-permute-start.15 = (bf16[16,3072]{1,0:T(8,128)(2,1)S(1)}, bf16[16,3072]{1,0:T(8,128)(2,1)S(1)}, u32[]{:S(2)}, u32[]{:S(2)}) collective-permute-start(bf16[16,3072]{1,0:T(8,128)(2,1)S(1)} %collective-permute-done.14.refs_6_), channel_id=1, source_target_pairs={{0,1},{1,0},{2,3},{3,2},{16,17},{17,16},{18,19},{19,18},{4,5},{5,4... | collective-permute-start | bytes 294920 | tf_op jit(solution)/shard_map/ppermute | solution.py:20
  46.5 4.5 %collective-permute-start.20 = (bf16[32,1152]{1,0:T(8,128)(2,1)S(1)}, bf16[32,1152]{1,0:T(8,128)(2,1)S(1)}, u32[]{:S(2)}, u32[]{:S(2)}) collective-permute-start(bf16[32,1152]{1,0:T(8,128)(2,1)S(1)} %get-tuple-element.57), channel_id=1, source_target_pairs={{0,4},{4,0},{8,12},{12,8},{1,5},{5,1},{9,13},{13,9},{2,6},{6,2},{1... | collective-permute-start | bytes 221192 | tf_op jit(solution)/shard_map/ppermute | solution.py:20
  48.3 5.3 %collective-permute-start.17 = (bf16[32,1152]{1,0:T(8,128)(2,1)S(1)}, bf16[32,1152]{1,0:T(8,128)(2,1)S(1)}, u32[]{:S(2)}, u32[]{:S(2)}) collective-permute-start(bf16[32,1152]{1,0:T(8,128)(2,1)S(1)} %get-tuple-element.51), channel_id=1, source_target_pairs={{0,4},{4,0},{8,12},{12,8},{1,5},{5,1},{9,13},{13,9},{2,6},{6,2},{1... | collective-permute-start | bytes 221192 | tf_op jit(solution)/shard_map/ppermute | solution.py:20
  51.0 7.7 %collective-permute-start.21 = (bf16[32,1152]{1,0:T(8,128)(2,1)S(1)}, bf16[32,1152]{1,0:T(8,128)(2,1)S(1)}, u32[]{:S(2)}, u32[]{:S(2)}) collective-permute-start(bf16[32,1152]{1,0:T(8,128)(2,1)S(1)} %get-tuple-element.59), channel_id=1, source_target_pairs={{0,8},{4,12},{8,0},{12,4},{1,9},{5,13},{9,1},{13,5},{2,10},{6,14},... | collective-permute-start | bytes 221192 | tf_op jit(solution)/shard_map/ppermute | solution.py:20
  52.0 6.7 %collective-permute-start.22 = (bf16[32,1152]{1,0:T(8,128)(2,1)S(1)}, bf16[32,1152]{1,0:T(8,128)(2,1)S(1)}, u32[]{:S(2)}, u32[]{:S(2)}) collective-permute-start(bf16[32,1152]{1,0:T(8,128)(2,1)S(1)} %get-tuple-element.60), channel_id=1, source_target_pairs={{0,4},{4,0},{8,12},{12,8},{1,5},{5,1},{9,13},{13,9},{2,6},{6,2},{1... | collective-permute-start | bytes 221192 | tf_op jit(solution)/shard_map/ppermute | solution.py:20
  53.7 6.6 %collective-permute-start.18 = (bf16[32,1152]{1,0:T(8,128)(2,1)S(1)}, bf16[32,1152]{1,0:T(8,128)(2,1)S(1)}, u32[]{:S(2)}, u32[]{:S(2)}) collective-permute-start(bf16[32,1152]{1,0:T(8,128)(2,1)S(1)} %get-tuple-element.53), channel_id=1, source_target_pairs={{0,8},{4,12},{8,0},{12,4},{1,9},{5,13},{9,1},{13,5},{2,10},{6,14},... | collective-permute-start | bytes 221192 | tf_op jit(solution)/shard_map/ppermute | solution.py:20
  55.8 4.7 %collective-permute-start.19 = (bf16[32,1152]{1,0:T(8,128)(2,1)S(1)}, bf16[32,1152]{1,0:T(8,128)(2,1)S(1)}, u32[]{:S(2)}, u32[]{:S(2)}) collective-permute-start(bf16[32,1152]{1,0:T(8,128)(2,1)S(1)} %get-tuple-element.54), channel_id=1, source_target_pairs={{0,4},{4,0},{8,12},{12,8},{1,5},{5,1},{9,13},{13,9},{2,6},{6,2},{1... | collective-permute-start | bytes 221192 | tf_op jit(solution)/shard_map/ppermute | solution.py:20
  (3 other events, 30.5 us)
where the time goes:
time: 61.3 us; the launch traced here: 61.2 us
  starting transfers between devices  23.6 us (38%)
  Pallas kernels  18 us (29%)
  waiting for transfers between devices  17.9 us (29%)
  local copies, waits for them, and re-layouts  1.28 us (2%)
    ppermute x23, starting transfers between devices, swapped_with(): return lax.ppermute(value, axes, pairs)  23.6 us
    ppermute x23, waiting for transfers between devices, swapped_with(): return lax.ppermute(value, axes, pairs)  17.9 us
    pallas_call x1, Pallas kernels, project(): pl.pallas_call(functools.partial(project_kernel, dims, blocks, chunks), o...  6.77 us
    pallas_call x1, Pallas kernels, near(): pl.pallas_call(near_kernel, out_shape=(jax.ShapeDtypeStruct(array.shape,...  5.04 us
    pallas_call x2, Pallas kernels, mix(): pl.pallas_call(functools.partial(mix_kernel, dims, chunk, part), out_shap...  2.64 us
    pallas_call x1, Pallas kernels, attend(): pl.pallas_call(functools.partial(attend_kernel, (gx_count, owned, steps,...  1.81 us
    pallas_call x2, Pallas kernels, finish(): pl.pallas_call(functools.partial(finish_kernel, dims), grid=(1,), out_sha...  1.46 us
    unnamed x8, local copies, waits for them, and re-layouts  1.28 us
  transfers between devices with their start and end apart: 23, of which 15 were waited for; matrix products, arithmetic and copies ran while one was open for 0% of the time, Pallas kernels for 12%

commit v1 on v0

--- a/solution.py
+++ b/solution.py
@@ -28,6 +28,10 @@
         blocks = [jnp.where(turn, blocks[k ^ bit], blocks[k]) for k in range(count)]
         bit *= 2
     return blocks
+
+
+def padded(rows):
+    return (rows + 7) // 8 * 8
 
 
 def farther_first(count):
@@ -215,9 +219,9 @@
         total = total + other[...].astype(jnp.float32)
     rows = outs[0].shape[0]
     for g in range(count):
-        total_ref[g] = total[g * rows : (g + 1) * rows]
+        total_ref[g, pl.ds(0, rows)] = total[g * rows : (g + 1) * rows]
     for k in range(count):
-        outs[k][...] = total_ref[lax.axis_index("gx") ^ k].astype(jnp.bfloat16)
+        outs[k][...] = total_ref[lax.axis_index("gx") ^ k, pl.ds(0, rows)].astype(jnp.bfloat16)
 
 
 def collect(own, received, after, gx_count):
@@ -230,7 +234,7 @@
         in_specs=[vmem, pl.BlockSpec(memory_space=pl.ANY)]
         + [vmem] * len(received),
         out_specs=[vmem] * gx_count,
-        scratch_shapes=[pltpu.VMEM((gx_count, rows, cols), jnp.float32)],
+        scratch_shapes=[pltpu.VMEM((gx_count, padded(rows), cols), jnp.float32)],
         compiler_params=pltpu.CompilerParams(vmem_limit_bytes=8 * 1024 * 1024),
         name="collect",
     )(own, after, *received)
@@ -269,7 +273,7 @@
                     rows_ref[s, window, pl.ds(part * half, half)] = value[s * steps : (s + 1) * steps]
     step_of = lax.broadcasted_iota(jnp.int32, (count, 1), 0) % steps
     for s in range(owned):
-        queries = rows_ref[s].astype(jnp.bfloat16)
+        queries = rows_ref[s, pl.ds(0, count)].astype(jnp.bfloat16)
         cached = lax.dot_general(
             queries, keys_ref[s], (((1,), (1,)), ((), ())), preferred_element_type=jnp.float32
         )
@@ -292,7 +296,7 @@
             exp_fresh = jnp.exp(fresh[u] - highest)
             denom = denom + exp_fresh
             total = total + exp_fresh * new_values[row : row + 1]
-        result_ref[s] = total * (1.0 / denom)
+        result_ref[s, pl.ds(0, count)] = total * (1.0 / denom)
     for k in range(gx_count):
         for h in range(heads):
             window = pl.ds((k * heads + h) * steps, steps)
@@ -318,8 +322,8 @@
         in_specs=[vmem] * (5 + gx_count),
         out_specs=[vmem] * gx_count,
         scratch_shapes=[
-            pltpu.VMEM((owned, count, width), jnp.float32),
-            pltpu.VMEM((owned, count, width), jnp.float32),
+            pltpu.VMEM((owned, padded(count) + 8, width), jnp.float32),
+            pltpu.VMEM((owned, padded(count) + 8, width), jnp.float32),
         ],
         compiler_params=pltpu.CompilerParams(vmem_limit_bytes=12 * 1024 * 1024),
         cost_estimate=pl.CostEstimate(
@@ -334,8 +338,8 @@
 def order_kernel(distances, *refs):
     out_ref, sorted_ref = refs[-2:]
     for k, block in zip(distances, refs):
-        sorted_ref[lax.axis_index("gx") ^ k] = block[...].astype(jnp.float32)
-    parts = [sorted_ref[g] for g in range(len(distances))]
+        sorted_ref[lax.axis_index("gx") ^ k, pl.ds(0, block.shape[0])] = block[...].astype(jnp.float32)
+    parts = [sorted_ref[g, pl.ds(0, block.shape[0])] for g in range(len(distances))]
     out_ref[...] = jnp.concatenate(parts, axis=0).astype(out_ref.dtype)
 
 
@@ -349,7 +353,7 @@
         out_shape=jax.ShapeDtypeStruct((count * rows, cols), blocks[0].dtype),
         in_specs=[vmem] * count,
         out_specs=vmem,
-        scratch_shapes=[pltpu.VMEM((count, rows, cols), jnp.float32)],
+        scratch_shapes=[pltpu.VMEM((count, padded(rows), cols), jnp.float32)],
         compiler_params=pltpu.CompilerParams(vmem_limit_bytes=8 * 1024 * 1024),
         name="order",
     )(*[blocks[k] for k in distances])
@@ -358,17 +362,10 @@
 def mix_kernel(dims, chunk, part, weight_ref, *refs):
     batch_count, gx_count, high_count, block = dims
     count = 2 * batch_count * high_count
-    blocks, own_ref, sends, (rows_ref, sum_ref) = refs[:count][::-1], refs[count], refs[count + 1 : -2], refs[-2:]
+    blocks, own_ref, sends, sum_ref = refs[:count][::-1], refs[count], refs[count + 1 : -1], refs[-1]
     shards = gx_count // batch_count
     group = block // shards
-    for relative in range(2):
-        for db in range(batch_count):
-            for dh in range(high_count):
-                b, h = lax.axis_index("batch") ^ db, lax.axis_index("gh") ^ dh
-                at = ((relative * batch_count + b) * high_count + h) * block
-                source = blocks[(relative * batch_count + db) * high_count + dh]
-                rows_ref[pl.ds(pl.multiple_of(at, block), block)] = source[...]
-    lhs = rows_ref[...]
+    lhs = jnp.concatenate([ref[...] for ref in blocks], axis=0)
     first, out_cols = part
     for start in range(0, out_cols, chunk):
         size = min(chunk, out_cols - start)
@@ -382,8 +379,8 @@
             parts = []
             for relative in range(2):
                 for h in range(high_count):
-                    at = ((relative * batch_count + b) * high_count + h) * block + hi * group
-                    at = pl.multiple_of(at, group)
+                    at = (relative * batch_count + (b ^ lax.axis_index("batch"))) * high_count + h
+                    at = pl.multiple_of(at * block + hi * group, group)
                     parts.append(sum_ref[pl.ds(at, group), pl.ds(0, size)])
             piece = jnp.concatenate(parts, axis=0)
             target = own_ref if k == 0 else sends[k - 1]
@@ -407,7 +404,7 @@
         out_shape=shapes,
         in_specs=[vmem] * (1 + len(blocks)),
         out_specs=[vmem] * gx_count,
-        scratch_shapes=[pltpu.VMEM((rows, depth), jnp.bfloat16), pltpu.VMEM((rows, chunk), jnp.float32)],
+        scratch_shapes=[pltpu.VMEM((rows, chunk), jnp.float32)],
         compiler_params=pltpu.CompilerParams(vmem_limit_bytes=20 * 1024 * 1024),
         cost_estimate=pl.CostEstimate(
             flops=2 * rows * depth * out_cols, bytes_accessed=2 * depth * out_cols, transcendentals=0
@@ -458,8 +455,9 @@
             for other in received:
                 total = total + other[window].astype(jnp.float32)
             total = total.reshape(batch_count, owned, steps, out_cols).astype(jnp.bfloat16)
+            high = lax.axis_index("gh") ^ h
             for g in range(batch_count):
-                first = ((g * high_count + h) * 2 + low) * owned
+                first = ((g * high_count + high) * 2 + low) * owned
                 out_ref[pl.ds(first, owned)] = total[g]
 
 

time: 61.3 us -> 61.4 us (level)
  no operation moved by 1% of the time
where the time goes in v1:
time: 61.4 us; the launch traced here: 61.2 us
  starting transfers between devices  23.6 us (38%)
  Pallas kernels  18 us (29%)
  waiting for transfers between devices  17.9 us (29%)
  local copies, waits for them, and re-layouts  1.28 us (2%)
    ppermute x23, starting transfers between devices, swapped_with(): return lax.ppermute(value, axes, pairs)  23.6 us
    ppermute x23, waiting for transfers between devices, swapped_with(): return lax.ppermute(value, axes, pairs)  17.9 us
    pallas_call x1, Pallas kernels, project(): pl.pallas_call(functools.partial(project_kernel, dims, blocks, chunks), o...  6.77 us
    pallas_call x1, Pallas kernels, near(): pl.pallas_call(near_kernel, out_shape=(jax.ShapeDtypeStruct(array.shape,...  5.04 us
    pallas_call x2, Pallas kernels, mix(): pl.pallas_call(functools.partial(mix_kernel, dims, chunk, part), out_shap...  2.58 us
    pallas_call x1, Pallas kernels, attend(): pl.pallas_call(functools.partial(attend_kernel, (gx_count, owned, steps,...  1.81 us
    pallas_call x2, Pallas kernels, finish(): pl.pallas_call(functools.partial(finish_kernel, dims), grid=(1,), out_sha...  1.46 us
    unnamed x8, local copies, waits for them, and re-layouts  1.28 us
  transfers between devices with their start and end apart: 23, of which 15 were waited for; matrix products, arithmetic and copies ran while one was open for 0% of the time, Pallas kernels for 12%

profile of v1, /device:TPU:0, one launch (start us, length us, event | category | flops | bytes accessed | tf_op | source)
XLA Modules:
  0.0 61.2 jit_solution(10367014301187563956)
XLA Ops:
  0.0 6.8 %project.1 = (bf16[64,3200]{1,0:T(8,128)(2,1)}, bf16[64,3200]{1,0:T(8,128)(2,1)}) custom-call(bf16[64,2,2304]{2,1,0:T(2,128)(2,1)} %tokens_hbm.1, bf16[2304,3072]{1,0:T(8,128)(2,1)} %query_hbm.1, bf16[2304,128]{1,0:T(8,128)(2,1)} %pair_hbm.1), custom_call_target="tpu_custom_call" | custom-call | flops 1887436800 | bytes 14745600 | tf_op jit(solution)/shard_map/project/pallas_call | solution.py:120
  7.3 1.3 %copy-done.2 = bf16[64,3200]{1,0:T(8,128)(2,1)S(1)} copy-done((bf16[64,3200]{1,0:T(8,128)(2,1)S(1)}, bf16[64,3200]{1,0:T(8,128)(2,1)}, u32[]{:S(2)}) %copy-start.2) | copy-done | bytes 409624
  9.0 2.9 %collective-permute-start.1 = (bf16[16,3200]{1,0:T(8,128)(2,1)S(1)}, bf16[16,3200]{1,0:T(8,128)(2,1)S(1)}, u32[]{:S(2)}, u32[]{:S(2)}) collective-permute-start(bf16[16,3200]{1,0:T(8,128)(2,1)S(1)} %get-tuple-element.38), channel_id=1, source_target_pairs={{0,2},{1,3},{2,0},{3,1},{16,18},{17,19},{18,16},{19,17},{4,6},{5,7... | collective-permute-start | bytes 307208 | tf_op jit(solution)/shard_map/ppermute | solution.py:20
  11.9 1.5 %collective-permute-start.2 = (bf16[16,3200]{1,0:T(8,128)(2,1)S(1)}, bf16[16,3200]{1,0:T(8,128)(2,1)S(1)}, u32[]{:S(2)}, u32[]{:S(2)}) collective-permute-start(bf16[16,3200]{1,0:T(8,128)(2,1)S(1)} %get-tuple-element.39), channel_id=1, source_target_pairs={{0,16},{1,17},{2,18},{3,19},{16,0},{17,1},{18,2},{19,3},{4,20},{5,... | collective-permute-start | bytes 307208 | tf_op jit(solution)/shard_map/ppermute | solution.py:20
  13.5 5.0 %near.1 = (bf16[3072,2304]{1,0:T(8,128)(2,1)S(1)}, f32[8,128]{1,0:T(8,128)S(1)}) custom-call(f32[16,3200]{1,0:T(8,128)S(1)} %get-tuple-element.35.after_ref.own_ref, bf16[3072,2304]{1,0:T(8,128)(2,1)} %source_ref.1), custom_call_target="tpu_custom_call" | custom-call | bytes 28311552 | tf_op jit(solution)/shard_map/near/pallas_call | solution.py:155
  19.1 2.7 %collective-permute-start.4 = (bf16[4,3200]{1,0:T(4,128)(2,1)S(1)}, bf16[4,3200]{1,0:T(4,128)(2,1)S(1)}, u32[]{:S(2)}, u32[]{:S(2)}) collective-permute-start(bf16[4,3200]{1,0:T(4,128)(2,1)S(1)} %get-tuple-element.42), channel_id=1, source_target_pairs={{0,8},{4,12},{8,0},{12,4},{1,9},{5,13},{9,1},{13,5},{2,10},{6,14},... | collective-permute-start | bytes 76808 | tf_op jit(solution)/shard_map/ppermute | solution.py:20
  21.8 1.4 %collective-permute-start.5 = (bf16[4,3200]{1,0:T(4,128)(2,1)S(1)}, bf16[4,3200]{1,0:T(4,128)(2,1)S(1)}, u32[]{:S(2)}, u32[]{:S(2)}) collective-permute-start(bf16[4,3200]{1,0:T(4,128)(2,1)S(1)} %get-tuple-element.43), channel_id=1, source_target_pairs={{0,12},{4,8},{8,4},{12,0},{1,13},{5,9},{9,5},{13,1},{2,14},{6,10},... | collective-permute-start | bytes 76808 | tf_op jit(solution)/shard_map/ppermute | solution.py:20
  23.9 3.5 %collective-permute-done.5.refs_2_ = bf16[4,3200]{1,0:T(4,128)(2,1)S(1)} collective-permute-done((bf16[4,3200]{1,0:T(4,128)(2,1)S(1)}, bf16[4,3200]{1,0:T(4,128)(2,1)S(1)}, u32[]{:S(2)}, u32[]{:S(2)}) %collective-permute-start.5) | collective-permute-done | bytes 25632 | tf_op jit(solution)/shard_map/ppermute | solution.py:20
  27.4 1.8 %attend.1 = (bf16[4,3072]{1,0:T(4,128)(2,1)S(1)}, bf16[4,3072]{1,0:T(4,128)(2,1)S(1)}, bf16[4,3072]{1,0:T(4,128)(2,1)S(1)}, bf16[4,3072]{1,0:T(4,128)(2,1)S(1)}) custom-call(f32[2,1,2048]{2,1,0:T(1,128)S(1)} %compare_select_fusion.mask_ref, f32[2,2,128]{2,1,0:T(2,128)S(1)} %get-tuple-element.62.cos_ref, f32[2,2,128]{2,1,0:T(2,128)S(1)} %get-tuple-element.61.sin_ref, ...), custom_call_target="tpu_custom_call" | custom-call | flops 402653184 | bytes 4194304 | tf_op jit(solution)/shard_map/attend/pallas_call | solution.py:319
  29.2 1.3 %collective-permute-start.7 = (bf16[4,3072]{1,0:T(4,128)(2,1)S(1)}, bf16[4,3072]{1,0:T(4,128)(2,1)S(1)}, u32[]{:S(2)}, u32[]{:S(2)}) collective-permute-start(bf16[4,3072]{1,0:T(4,128)(2,1)S(1)} %get-tuple-element.46), channel_id=1, source_target_pairs={{0,8},{4,12},{8,0},{12,4},{1,9},{5,13},{9,1},{13,5},{2,10},{6,14},... | collective-permute-start | bytes 73736 | tf_op jit(solution)/shard_map/ppermute | solution.py:20
  31.5 1.3 %collective-permute-start.9 = (bf16[4,3072]{1,0:T(4,128)(2,1)S(1)}, bf16[4,3072]{1,0:T(4,128)(2,1)S(1)}, u32[]{:S(2)}, u32[]{:S(2)}) collective-permute-start(bf16[4,3072]{1,0:T(4,128)(2,1)S(1)} %get-tuple-element.48), channel_id=1, source_target_pairs={{0,4},{4,0},{8,12},{12,8},{1,5},{5,1},{9,13},{13,9},{2,6},{6,2},{1... | collective-permute-start | bytes 73736 | tf_op jit(solution)/shard_map/ppermute | solution.py:20
  32.8 1.2 %collective-permute-done.7.refs_1_ = bf16[4,3072]{1,0:T(4,128)(2,1)S(1)} collective-permute-done((bf16[4,3072]{1,0:T(4,128)(2,1)S(1)}, bf16[4,3072]{1,0:T(4,128)(2,1)S(1)}, u32[]{:S(2)}, u32[]{:S(2)}) %collective-permute-start.7) | collective-permute-done | bytes 24608 | tf_op jit(solution)/shard_map/ppermute | solution.py:20
  34.0 2.1 %collective-permute-done.8.refs_2_ = bf16[4,3072]{1,0:T(4,128)(2,1)S(1)} collective-permute-done((bf16[4,3072]{1,0:T(4,128)(2,1)S(1)}, bf16[4,3072]{1,0:T(4,128)(2,1)S(1)}, u32[]{:S(2)}, u32[]{:S(2)}) %collective-permute-start.8) | collective-permute-done | bytes 24608 | tf_op jit(solution)/shard_map/ppermute | solution.py:20
  36.3 2.5 %collective-permute-start.10 = (bf16[16,3072]{1,0:T(8,128)(2,1)S(1)}, bf16[16,3072]{1,0:T(8,128)(2,1)S(1)}, u32[]{:S(2)}, u32[]{:S(2)}) collective-permute-start(bf16[16,3072]{1,0:T(8,128)(2,1)S(1)} %order.1.refs_7_), channel_id=1, source_target_pairs={{0,18},{1,19},{2,16},{3,17},{16,2},{17,3},{18,0},{19,1},{4,22},{5,... | collective-permute-start | bytes 294920 | tf_op jit(solution)/shard_map/ppermute | solution.py:20
  39.8 2.0 %collective-permute-done.10.refs_4_ = bf16[16,3072]{1,0:T(8,128)(2,1)S(1)} collective-permute-done((bf16[16,3072]{1,0:T(8,128)(2,1)S(1)}, bf16[16,3072]{1,0:T(8,128)(2,1)S(1)}, u32[]{:S(2)}, u32[]{:S(2)}) %collective-permute-start.10) | collective-permute-done | bytes 98336 | tf_op jit(solution)/shard_map/ppermute | solution.py:20
  41.8 1.5 %collective-permute-done.12.refs_5_ = bf16[16,3072]{1,0:T(8,128)(2,1)S(1)} collective-permute-done((bf16[16,3072]{1,0:T(8,128)(2,1)S(1)}, bf16[16,3072]{1,0:T(8,128)(2,1)S(1)}, u32[]{:S(2)}, u32[]{:S(2)}) %collective-permute-start.12) | collective-permute-done | bytes 98336 | tf_op jit(solution)/shard_map/ppermute | solution.py:20
  45.2 1.3 %mix.3 = (f32[32,1152]{1,0:T(8,128)S(1)}, bf16[32,1152]{1,0:T(8,128)(2,1)S(1)}, f32[32,1152]{1,0:T(8,128)S(1)}, bf16[32,1152]{1,0:T(8,128)(2,1)S(1)}) custom-call(bf16[3072,2304]{1,0:T(8,128)(2,1)S(1)} %get-tuple-element.36.weight_ref, bf16[16,3072]{1,0:T(8,128)(2,1)S(1)} %collective-permute-done.11.refs_0_, ...), custom_call_target="tpu_custom_call" | custom-call | flops 905969664 | bytes 7077888 | tf_op jit(solution)/shard_map/mix/pallas_call | solution.py:402
  47.0 1.3 %mix.2 = (f32[32,1152]{1,0:T(8,128)S(1)}, bf16[32,1152]{1,0:T(8,128)(2,1)S(1)}, f32[32,1152]{1,0:T(8,128)S(1)}, bf16[32,1152]{1,0:T(8,128)(2,1)S(1)}) custom-call(bf16[3072,2304]{1,0:T(8,128)(2,1)S(1)} %get-tuple-element.36.weight_ref, bf16[16,3072]{1,0:T(8,128)(2,1)S(1)} %collective-permute-done.11.refs_0_, ...), custom_call_target="tpu_custom_call" | custom-call | flops 905969664 | bytes 7077888 | tf_op jit(solution)/shard_map/mix/pallas_call | solution.py:402
  48.3 1.6 %collective-permute-start.17 = (bf16[32,1152]{1,0:T(8,128)(2,1)S(1)}, bf16[32,1152]{1,0:T(8,128)(2,1)S(1)}, u32[]{:S(2)}, u32[]{:S(2)}) collective-permute-start(bf16[32,1152]{1,0:T(8,128)(2,1)S(1)} %get-tuple-element.51), channel_id=1, source_target_pairs={{0,4},{4,0},{8,12},{12,8},{1,5},{5,1},{9,13},{13,9},{2,6},{6,2},{1... | collective-permute-start | bytes 221192 | tf_op jit(solution)/shard_map/ppermute | solution.py:20
  49.9 1.1 %collective-permute-done.20.taken_ref = bf16[32,1152]{1,0:T(8,128)(2,1)S(1)} collective-permute-done((bf16[32,1152]{1,0:T(8,128)(2,1)S(1)}, bf16[32,1152]{1,0:T(8,128)(2,1)S(1)}, u32[]{:S(2)}, u32[]{:S(2)}) %collective-permute-start.20) | collective-permute-done | bytes 73760 | tf_op jit(solution)/shard_map/ppermute | solution.py:20
  51.1 1.0 %collective-permute-start.21 = (bf16[32,1152]{1,0:T(8,128)(2,1)S(1)}, bf16[32,1152]{1,0:T(8,128)(2,1)S(1)}, u32[]{:S(2)}, u32[]{:S(2)}) collective-permute-start(bf16[32,1152]{1,0:T(8,128)(2,1)S(1)} %get-tuple-element.59), channel_id=1, source_target_pairs={{0,8},{4,12},{8,0},{12,4},{1,9},{5,13},{9,1},{13,5},{2,10},{6,14},... | collective-permute-start | bytes 221192 | tf_op jit(solution)/shard_map/ppermute | solution.py:20
  52.0 1.7 %collective-permute-start.22 = (bf16[32,1152]{1,0:T(8,128)(2,1)S(1)}, bf16[32,1152]{1,0:T(8,128)(2,1)S(1)}, u32[]{:S(2)}, u32[]{:S(2)}) collective-permute-start(bf16[32,1152]{1,0:T(8,128)(2,1)S(1)} %get-tuple-element.60), channel_id=1, source_target_pairs={{0,4},{4,0},{8,12},{12,8},{1,5},{5,1},{9,13},{13,9},{2,6},{6,2},{1... | collective-permute-start | bytes 221192 | tf_op jit(solution)/shard_map/ppermute | solution.py:20
  53.7 2.0 %collective-permute-start.18 = (bf16[32,1152]{1,0:T(8,128)(2,1)S(1)}, bf16[32,1152]{1,0:T(8,128)(2,1)S(1)}, u32[]{:S(2)}, u32[]{:S(2)}) collective-permute-start(bf16[32,1152]{1,0:T(8,128)(2,1)S(1)} %get-tuple-element.53), channel_id=1, source_target_pairs={{0,8},{4,12},{8,0},{12,4},{1,9},{5,13},{9,1},{13,5},{2,10},{6,14},... | collective-permute-start | bytes 221192 | tf_op jit(solution)/shard_map/ppermute | solution.py:20
  56.2 2.5 %collective-permute-done.21.refs_0_ = bf16[32,1152]{1,0:T(8,128)(2,1)S(1)} collective-permute-done((bf16[32,1152]{1,0:T(8,128)(2,1)S(1)}, bf16[32,1152]{1,0:T(8,128)(2,1)S(1)}, u32[]{:S(2)}, u32[]{:S(2)}) %collective-permute-start.21) | collective-permute-done | bytes 73760 | tf_op jit(solution)/shard_map/ppermute | solution.py:20
  (47 shorter events, 9.7 us)
Async XLA Ops:
  6.8 20.6 %copy-start = (bf16[2,2048,256]{2,1,0:T(8,128)(2,1)S(1)}, bf16[2,2048,256]{2,1,0:T(8,128)(2,1)}, u32[]{:S(2)}) copy-start(bf16[2,2048,256]{2,1,0:T(8,128)(2,1)} %keys_ref.1) | copy-start | bytes 6291460
  6.8 2.1 %collective-permute-start = (bf16[64,3200]{1,0:T(8,128)(2,1)}, bf16[64,3200]{1,0:T(8,128)(2,1)S(1)}, u32[]{:S(2)}, u32[]{:S(2)}) collective-permute-start(bf16[64,3200]{1,0:T(8,128)(2,1)} %get-tuple-element.34), channel_id=1, source_target_pairs={{0,1},{1,0},{2,3},{3,2},{16,17},{17,16},{18,19},{19,18},{4,5},{5,4... | collective-permute-start | bytes 1228808 | tf_op jit(solution)/shard_map/ppermute | solution.py:20
  9.0 9.5 %collective-permute-start.1 = (bf16[16,3200]{1,0:T(8,128)(2,1)S(1)}, bf16[16,3200]{1,0:T(8,128)(2,1)S(1)}, u32[]{:S(2)}, u32[]{:S(2)}) collective-permute-start(bf16[16,3200]{1,0:T(8,128)(2,1)S(1)} %get-tuple-element.38), channel_id=1, source_target_pairs={{0,2},{1,3},{2,0},{3,1},{16,18},{17,19},{18,16},{19,17},{4,6},{5,7... | collective-permute-start | bytes 307208 | tf_op jit(solution)/shard_map/ppermute | solution.py:20
  11.9 6.6 %collective-permute-start.2 = (bf16[16,3200]{1,0:T(8,128)(2,1)S(1)}, bf16[16,3200]{1,0:T(8,128)(2,1)S(1)}, u32[]{:S(2)}, u32[]{:S(2)}) collective-permute-start(bf16[16,3200]{1,0:T(8,128)(2,1)S(1)} %get-tuple-element.39), channel_id=1, source_target_pairs={{0,16},{1,17},{2,18},{3,19},{16,0},{17,1},{18,2},{19,3},{4,20},{5,... | collective-permute-start | bytes 307208 | tf_op jit(solution)/shard_map/ppermute | solution.py:20
  13.5 5.6 %collective-permute-start.3 = (bf16[16,3200]{1,0:T(8,128)(2,1)S(1)}, bf16[16,3200]{1,0:T(8,128)(2,1)S(1)}, u32[]{:S(2)}, u32[]{:S(2)}) collective-permute-start(bf16[16,3200]{1,0:T(8,128)(2,1)S(1)} %get-tuple-element.40), channel_id=1, source_target_pairs={{0,18},{1,19},{2,16},{3,17},{16,2},{17,3},{18,0},{19,1},{4,22},{5,... | collective-permute-start | bytes 307208 | tf_op jit(solution)/shard_map/ppermute | solution.py:20
  19.1 4.8 %collective-permute-start.4 = (bf16[4,3200]{1,0:T(4,128)(2,1)S(1)}, bf16[4,3200]{1,0:T(4,128)(2,1)S(1)}, u32[]{:S(2)}, u32[]{:S(2)}) collective-permute-start(bf16[4,3200]{1,0:T(4,128)(2,1)S(1)} %get-tuple-element.42), channel_id=1, source_target_pairs={{0,8},{4,12},{8,0},{12,4},{1,9},{5,13},{9,1},{13,5},{2,10},{6,14},... | collective-permute-start | bytes 76808 | tf_op jit(solution)/shard_map/ppermute | solution.py:20
  21.8 5.6 %collective-permute-start.5 = (bf16[4,3200]{1,0:T(4,128)(2,1)S(1)}, bf16[4,3200]{1,0:T(4,128)(2,1)S(1)}, u32[]{:S(2)}, u32[]{:S(2)}) collective-permute-start(bf16[4,3200]{1,0:T(4,128)(2,1)S(1)} %get-tuple-element.43), channel_id=1, source_target_pairs={{0,12},{4,8},{8,4},{12,0},{1,13},{5,9},{9,5},{13,1},{2,14},{6,10},... | collective-permute-start | bytes 76808 | tf_op jit(solution)/shard_map/ppermute | solution.py:20
  23.1 4.3 %collective-permute-start.6 = (bf16[4,3200]{1,0:T(4,128)(2,1)S(1)}, bf16[4,3200]{1,0:T(4,128)(2,1)S(1)}, u32[]{:S(2)}, u32[]{:S(2)}) collective-permute-start(bf16[4,3200]{1,0:T(4,128)(2,1)S(1)} %get-tuple-element.44), channel_id=1, source_target_pairs={{0,4},{4,0},{8,12},{12,8},{1,5},{5,1},{9,13},{13,9},{2,6},{6,2},{1... | collective-permute-start | bytes 76808 | tf_op jit(solution)/shard_map/ppermute | solution.py:20
  29.2 4.8 %collective-permute-start.7 = (bf16[4,3072]{1,0:T(4,128)(2,1)S(1)}, bf16[4,3072]{1,0:T(4,128)(2,1)S(1)}, u32[]{:S(2)}, u32[]{:S(2)}) collective-permute-start(bf16[4,3072]{1,0:T(4,128)(2,1)S(1)} %get-tuple-element.46), channel_id=1, source_target_pairs={{0,8},{4,12},{8,0},{12,4},{1,9},{5,13},{9,1},{13,5},{2,10},{6,14},... | collective-permute-start | bytes 73736 | tf_op jit(solution)/shard_map/ppermute | solution.py:20
  30.5 5.6 %collective-permute-start.8 = (bf16[4,3072]{1,0:T(4,128)(2,1)S(1)}, bf16[4,3072]{1,0:T(4,128)(2,1)S(1)}, u32[]{:S(2)}, u32[]{:S(2)}) collective-permute-start(bf16[4,3072]{1,0:T(4,128)(2,1)S(1)} %get-tuple-element.47), channel_id=1, source_target_pairs={{0,12},{4,8},{8,4},{12,0},{1,13},{5,9},{9,5},{13,1},{2,14},{6,10},... | collective-permute-start | bytes 73736 | tf_op jit(solution)/shard_map/ppermute | solution.py:20
  31.5 4.7 %collective-permute-start.9 = (bf16[4,3072]{1,0:T(4,128)(2,1)S(1)}, bf16[4,3072]{1,0:T(4,128)(2,1)S(1)}, u32[]{:S(2)}, u32[]{:S(2)}) collective-permute-start(bf16[4,3072]{1,0:T(4,128)(2,1)S(1)} %get-tuple-element.48), channel_id=1, source_target_pairs={{0,4},{4,0},{8,12},{12,8},{1,5},{5,1},{9,13},{13,9},{2,6},{6,2},{1... | collective-permute-start | bytes 73736 | tf_op jit(solution)/shard_map/ppermute | solution.py:20
  36.3 5.6 %collective-permute-start.10 = (bf16[16,3072]{1,0:T(8,128)(2,1)S(1)}, bf16[16,3072]{1,0:T(8,128)(2,1)S(1)}, u32[]{:S(2)}, u32[]{:S(2)}) collective-permute-start(bf16[16,3072]{1,0:T(8,128)(2,1)S(1)} %order.1.refs_7_), channel_id=1, source_target_pairs={{0,18},{1,19},{2,16},{3,17},{16,2},{17,3},{18,0},{19,1},{4,22},{5,... | collective-permute-start | bytes 294920 | tf_op jit(solution)/shard_map/ppermute | solution.py:20
  38.8 4.6 %collective-permute-start.12 = (bf16[16,3072]{1,0:T(8,128)(2,1)S(1)}, bf16[16,3072]{1,0:T(8,128)(2,1)S(1)}, u32[]{:S(2)}, u32[]{:S(2)}) collective-permute-start(bf16[16,3072]{1,0:T(8,128)(2,1)S(1)} %order.1.refs_7_), channel_id=1, source_target_pairs={{0,16},{1,17},{2,18},{3,19},{16,0},{17,1},{18,2},{19,3},{4,20},{5,... | collective-permute-start | bytes 294920 | tf_op jit(solution)/shard_map/ppermute | solution.py:20
  39.3 4.6 %collective-permute-start.14 = (bf16[16,3072]{1,0:T(8,128)(2,1)S(1)}, bf16[16,3072]{1,0:T(8,128)(2,1)S(1)}, u32[]{:S(2)}, u32[]{:S(2)}) collective-permute-start(bf16[16,3072]{1,0:T(8,128)(2,1)S(1)} %order.1.refs_7_), channel_id=1, source_target_pairs={{0,2},{1,3},{2,0},{3,1},{16,18},{17,19},{18,16},{19,17},{4,6},{5,7... | collective-permute-start | bytes 294920 | tf_op jit(solution)/shard_map/ppermute | solution.py:20
  39.8 4.1 %collective-permute-start.16 = (bf16[16,3072]{1,0:T(8,128)(2,1)S(1)}, bf16[16,3072]{1,0:T(8,128)(2,1)S(1)}, u32[]{:S(2)}, u32[]{:S(2)}) collective-permute-start(bf16[16,3072]{1,0:T(8,128)(2,1)S(1)} %order.1.refs_7_), channel_id=1, source_target_pairs={{0,1},{1,0},{2,3},{3,2},{16,17},{17,16},{18,19},{19,18},{4,5},{5,4... | collective-permute-start | bytes 294920 | tf_op jit(solution)/shard_map/ppermute | solution.py:20
  41.8 2.1 %collective-permute-start.11 = (bf16[16,3072]{1,0:T(8,128)(2,1)S(1)}, bf16[16,3072]{1,0:T(8,128)(2,1)S(1)}, u32[]{:S(2)}, u32[]{:S(2)}) collective-permute-start(bf16[16,3072]{1,0:T(8,128)(2,1)S(1)} %collective-permute-done.10.refs_4_), channel_id=1, source_target_pairs={{0,1},{1,0},{2,3},{3,2},{16,17},{17,16},{18,19},{19,18},{4,5},{5,4... | collective-permute-start | bytes 294920 | tf_op jit(solution)/shard_map/ppermute | solution.py:20
  43.4 1.3 %collective-permute-start.13 = (bf16[16,3072]{1,0:T(8,128)(2,1)S(1)}, bf16[16,3072]{1,0:T(8,128)(2,1)S(1)}, u32[]{:S(2)}, u32[]{:S(2)}) collective-permute-start(bf16[16,3072]{1,0:T(8,128)(2,1)S(1)} %collective-permute-done.12.refs_5_), channel_id=1, source_target_pairs={{0,1},{1,0},{2,3},{3,2},{16,17},{17,16},{18,19},{19,18},{4,5},{5,4... | collective-permute-start | bytes 294920 | tf_op jit(solution)/shard_map/ppermute | solution.py:20
  43.9 1.3 %collective-permute-start.15 = (bf16[16,3072]{1,0:T(8,128)(2,1)S(1)}, bf16[16,3072]{1,0:T(8,128)(2,1)S(1)}, u32[]{:S(2)}, u32[]{:S(2)}) collective-permute-start(bf16[16,3072]{1,0:T(8,128)(2,1)S(1)} %collective-permute-done.14.refs_6_), channel_id=1, source_target_pairs={{0,1},{1,0},{2,3},{3,2},{16,17},{17,16},{18,19},{19,18},{4,5},{5,4... | collective-permute-start | bytes 294920 | tf_op jit(solution)/shard_map/ppermute | solution.py:20
  46.5 4.5 %collective-permute-start.20 = (bf16[32,1152]{1,0:T(8,128)(2,1)S(1)}, bf16[32,1152]{1,0:T(8,128)(2,1)S(1)}, u32[]{:S(2)}, u32[]{:S(2)}) collective-permute-start(bf16[32,1152]{1,0:T(8,128)(2,1)S(1)} %get-tuple-element.57), channel_id=1, source_target_pairs={{0,4},{4,0},{8,12},{12,8},{1,5},{5,1},{9,13},{13,9},{2,6},{6,2},{1... | collective-permute-start | bytes 221192 | tf_op jit(solution)/shard_map/ppermute | solution.py:20
  48.3 5.4 %collective-permute-start.17 = (bf16[32,1152]{1,0:T(8,128)(2,1)S(1)}, bf16[32,1152]{1,0:T(8,128)(2,1)S(1)}, u32[]{:S(2)}, u32[]{:S(2)}) collective-permute-start(bf16[32,1152]{1,0:T(8,128)(2,1)S(1)} %get-tuple-element.51), channel_id=1, source_target_pairs={{0,4},{4,0},{8,12},{12,8},{1,5},{5,1},{9,13},{13,9},{2,6},{6,2},{1... | collective-permute-start | bytes 221192 | tf_op jit(solution)/shard_map/ppermute | solution.py:20
  51.1 7.7 %collective-permute-start.21 = (bf16[32,1152]{1,0:T(8,128)(2,1)S(1)}, bf16[32,1152]{1,0:T(8,128)(2,1)S(1)}, u32[]{:S(2)}, u32[]{:S(2)}) collective-permute-start(bf16[32,1152]{1,0:T(8,128)(2,1)S(1)} %get-tuple-element.59), channel_id=1, source_target_pairs={{0,8},{4,12},{8,0},{12,4},{1,9},{5,13},{9,1},{13,5},{2,10},{6,14},... | collective-permute-start | bytes 221192 | tf_op jit(solution)/shard_map/ppermute | solution.py:20
  52.0 6.7 %collective-permute-start.22 = (bf16[32,1152]{1,0:T(8,128)(2,1)S(1)}, bf16[32,1152]{1,0:T(8,128)(2,1)S(1)}, u32[]{:S(2)}, u32[]{:S(2)}) collective-permute-start(bf16[32,1152]{1,0:T(8,128)(2,1)S(1)} %get-tuple-element.60), channel_id=1, source_target_pairs={{0,4},{4,0},{8,12},{12,8},{1,5},{5,1},{9,13},{13,9},{2,6},{6,2},{1... | collective-permute-start | bytes 221192 | tf_op jit(solution)/shard_map/ppermute | solution.py:20
  53.7 6.6 %collective-permute-start.18 = (bf16[32,1152]{1,0:T(8,128)(2,1)S(1)}, bf16[32,1152]{1,0:T(8,128)(2,1)S(1)}, u32[]{:S(2)}, u32[]{:S(2)}) collective-permute-start(bf16[32,1152]{1,0:T(8,128)(2,1)S(1)} %get-tuple-element.53), channel_id=1, source_target_pairs={{0,8},{4,12},{8,0},{12,4},{1,9},{5,13},{9,1},{13,5},{2,10},{6,14},... | collective-permute-start | bytes 221192 | tf_op jit(solution)/shard_map/ppermute | solution.py:20
  55.7 4.8 %collective-permute-start.19 = (bf16[32,1152]{1,0:T(8,128)(2,1)S(1)}, bf16[32,1152]{1,0:T(8,128)(2,1)S(1)}, u32[]{:S(2)}, u32[]{:S(2)}) collective-permute-start(bf16[32,1152]{1,0:T(8,128)(2,1)S(1)} %get-tuple-element.54), channel_id=1, source_target_pairs={{0,4},{4,0},{8,12},{12,8},{1,5},{5,1},{9,13},{13,9},{2,6},{6,2},{1... | collective-permute-start | bytes 221192 | tf_op jit(solution)/shard_map/ppermute | solution.py:20
  (3 other events, 30.5 us)

commit v2 on v1

--- a/solution.py
+++ b/solution.py
@@ -413,74 +413,97 @@
     )(w_out, *blocks[::-1])
 
 
-def relay_kernel(own_ref, taken_ref, near_ref, sum_ref, copy_ref):
+def relay_kernel(own_ref, taken_ref, out_ref):
     total = own_ref[...] + taken_ref[...].astype(jnp.float32)
-    sum_ref[...] = total.astype(sum_ref.dtype)
-    copy_ref[...] = near_ref[...]
-
-
-def relay(own, taken, near):
+    out_ref[...] = total.astype(out_ref.dtype)
+
+
+def relay(own, taken, kind):
     vmem = pl.BlockSpec(memory_space=pltpu.VMEM)
     return pl.pallas_call(
         relay_kernel,
-        out_shape=[jax.ShapeDtypeStruct(near.shape, near.dtype)] * 2,
-        in_specs=[vmem] * 3,
-        out_specs=[vmem] * 2,
+        out_shape=jax.ShapeDtypeStruct(taken.shape, kind),
+        in_specs=[vmem, vmem],
+        out_specs=vmem,
         compiler_params=pltpu.CompilerParams(vmem_limit_bytes=8 * 1024 * 1024),
         name="relay",
-    )(own, taken, near)
-
-
-def summed_terms(sends):
-    count = len(sends) + 1
+    )(own, taken)
+
+
+def held_kernel(after_ref, source_ref, out_ref):
+    out_ref[...] = source_ref[...]
+
+
+def held(array, after):
+    vmem = pl.BlockSpec(memory_space=pltpu.VMEM)
+    return pl.pallas_call(
+        held_kernel,
+        out_shape=jax.ShapeDtypeStruct(array.shape, array.dtype),
+        in_specs=[pl.BlockSpec(memory_space=pl.ANY), vmem],
+        out_specs=vmem,
+        compiler_params=pltpu.CompilerParams(vmem_limit_bytes=8 * 1024 * 1024),
+        name="held",
+    )(after, array)
+
+
+def summed_terms(products):
+    count = len(products[0])
     if count != 4:
-        return [swapped_with(sends[k - 1], "gx", (count,), (k,)) for k in farther_first(count)[1:]]
-    near, far, farthest = sends
-    taken = swapped_with(farthest, "gx", (count,), (1,))
-    both, near = relay(far, taken, near)
-    return [swapped_with(both, "gx", (count,), (2,)), swapped_with(near, "gx", (count,), (1,))]
-
-
-def finish_kernel(dims, own_ref, *refs):
-    received, out_ref = refs[: len(refs) - 1], refs[-1]
+        return [
+            [swapped_with(product[k], "gx", (count,), (k,)) for k in farther_first(count)[1:]]
+            for product in products
+        ]
+    boths = [
+        relay(product[2], swapped_with(product[3], "gx", (count,), (1,)), jnp.bfloat16)
+        for product in products
+    ]
+    return [
+        [
+            swapped_with(both, "gx", (count,), (2,)),
+            swapped_with(held(product[1], boths[-1]), "gx", (count,), (1,)),
+        ]
+        for both, product in zip(boths, products)
+    ]
+
+
+def finish_kernel(dims, counts, *refs):
+    refs, out_ref = list(refs[:-1]), refs[-1]
     batch_count, high_count, owned = dims
-    steps, out_cols = out_ref.shape[1:]
+    steps = out_ref.shape[1]
     size = batch_count * owned * steps
-    received = [ref for ref in received if ref.shape == own_ref.shape]
-    for relative in range(2):
-        low = lax.axis_index("gl") ^ relative
-        for h in range(high_count):
-            window = pl.ds((relative * high_count + h) * size, size)
-            total = own_ref[window]
-            for other in received:
-                total = total + other[window].astype(jnp.float32)
-            total = total.reshape(batch_count, owned, steps, out_cols).astype(jnp.bfloat16)
-            high = lax.axis_index("gh") ^ h
-            for g in range(batch_count):
-                first = ((g * high_count + high) * 2 + low) * owned
-                out_ref[pl.ds(first, owned)] = total[g]
-
-
-def finish(own, received, dims, steps, part, parts, before):
-    rows, out_cols = own.shape
-    whole = pl.BlockSpec((rows, out_cols), lambda step: (0, 0))
-    operands = [own, *received]
-    in_specs = [whole] * len(operands)
-    aliases = {}
-    if before is not None:
-        aliases[len(operands)] = 0
-        operands.append(before)
-        in_specs.append(pl.BlockSpec(memory_space=pl.ANY))
-    return pl.pallas_call(
-        functools.partial(finish_kernel, dims),
-        grid=(1,),
-        out_shape=jax.ShapeDtypeStruct((rows // steps, steps, out_cols * parts), jnp.bfloat16),
-        in_specs=in_specs,
-        out_specs=pl.BlockSpec((rows // steps, steps, out_cols), lambda step: (0, 0, part)),
-        input_output_aliases=aliases,
+    begin = 0
+    for count in counts:
+        own_ref, *received = refs[:count]
+        refs = refs[count:]
+        cols = own_ref.shape[1]
+        for relative in range(2):
+            low = lax.axis_index("gl") ^ relative
+            for h in range(high_count):
+                window = pl.ds((relative * high_count + h) * size, size)
+                total = own_ref[window]
+                for other in received:
+                    total = total + other[window].astype(jnp.float32)
+                total = total.reshape(batch_count, owned, steps, cols).astype(jnp.bfloat16)
+                high = lax.axis_index("gh") ^ h
+                for g in range(batch_count):
+                    first = ((g * high_count + high) * 2 + low) * owned
+                    out_ref[pl.ds(first, owned), :, pl.ds(begin, cols)] = total[g]
+        begin += cols
+
+
+def finish(parts, dims, steps):
+    vmem = pl.BlockSpec(memory_space=pltpu.VMEM)
+    rows = parts[0][0].shape[0]
+    out_cols = sum(part[0].shape[1] for part in parts)
+    terms = [term for part in parts for term in part]
+    return pl.pallas_call(
+        functools.partial(finish_kernel, dims, [len(part) for part in parts]),
+        out_shape=jax.ShapeDtypeStruct((rows // steps, steps, out_cols), jnp.bfloat16),
+        in_specs=[vmem] * len(terms),
+        out_specs=vmem,
         compiler_params=pltpu.CompilerParams(vmem_limit_bytes=16 * 1024 * 1024),
         name="finish",
-    )(*operands)
+    )(*terms)
 
 
 def local(tokens, w_query, w_keyval, w_out, cache_keys, cache_values, lengths):
@@ -517,15 +540,15 @@
     out_cols = w_out.shape[1]
     parts = 2 if out_cols % 256 == 0 else 1
     size = out_cols // parts
-    mixed = None
     products = [
         mix(ours + theirs, w_out, (batch_count, gx_count, high_count, rows_here), (part * size, size))
         for part in range(parts)
     ]
-    for part, (own, *sends) in enumerate(products):
-        received = summed_terms(sends)
-        mixed = finish(own, received, (batch_count, high_count, owned), steps, part, parts, mixed)
-    return mixed
+    summands = [[product[0], *terms] for product, terms in zip(products, summed_terms(products))]
+    for part in range(parts - 1):
+        own, both, *rest = summands[part]
+        summands[part] = [relay(own, both, jnp.float32), *rest]
+    return finish(summands, (batch_count, high_count, owned), steps)
 
 
 def solution(mesh):

time: 61.4 us -> 62.2 us (1.013)
  waiting for transfers between devices: 17.9 us -> 18.6 us
  starting transfers between devices: 23.6 us -> 24.3 us
    ppermute x23, starting transfers between devices: 23.6 us -> 24.3 us  [swapped_with(): return lax.ppermute(value, axes, pairs)]
    pallas_call x4 -> x6, Pallas kernels: 1.51 us -> 0.91 us  [the longest x1 0.84 us: finish(): pl.pallas_call(functools.partial(finish_kernel, dims, [len(part) for part...]
  transfers between devices with their start and end apart: 23 -> 23, of which waited for: 15 -> 16; matrix products, arithmetic and copies ran while one was open for 0% -> 0% of each run, Pallas kernels for 12% -> 10%
where the time goes in v2:
time: 62.2 us; the launch traced here: 62 us
  starting transfers between devices  24.3 us (39%)
  waiting for transfers between devices  18.6 us (30%)
  Pallas kernels  17.4 us (28%)
  local copies, waits for them, and re-layouts  1.28 us (2%)
    ppermute x23, starting transfers between devices, swapped_with(): return lax.ppermute(value, axes, pairs)  24.3 us
    ppermute x23, waiting for transfers between devices, swapped_with(): return lax.ppermute(value, axes, pairs)  18.6 us
    pallas_call x1, Pallas kernels, project(): pl.pallas_call(functools.partial(project_kernel, dims, blocks, chunks), o...  6.78 us
    pallas_call x1, Pallas kernels, near(): pl.pallas_call(near_kernel, out_shape=(jax.ShapeDtypeStruct(array.shape,...  5.04 us
    pallas_call x2, Pallas kernels, mix(): pl.pallas_call(functools.partial(mix_kernel, dims, chunk, part), out_shap...  2.58 us
    pallas_call x1, Pallas kernels, attend(): pl.pallas_call(functools.partial(attend_kernel, (gx_count, owned, steps,...  1.81 us
    unnamed x8, local copies, waits for them, and re-layouts  1.28 us
  transfers between devices with their start and end apart: 23, of which 16 were waited for; matrix products, arithmetic and copies ran while one was open for 0% of the time, Pallas kernels for 10%

profile of v2, /device:TPU:0, one launch (start us, length us, event | category | flops | bytes accessed | tf_op | source)
XLA Modules:
  0.0 62.0 jit_solution(8687618805913113471)
XLA Ops:
  0.0 6.8 %project.1 = (bf16[64,3200]{1,0:T(8,128)(2,1)}, bf16[64,3200]{1,0:T(8,128)(2,1)}) custom-call(bf16[64,2,2304]{2,1,0:T(2,128)(2,1)} %tokens_hbm.1, bf16[2304,3072]{1,0:T(8,128)(2,1)} %query_hbm.1, bf16[2304,128]{1,0:T(8,128)(2,1)} %pair_hbm.1), custom_call_target="tpu_custom_call" | custom-call | flops 1887436800 | bytes 14745600 | tf_op jit(solution)/shard_map/project/pallas_call | solution.py:120
  7.3 1.3 %copy-done.2 = bf16[64,3200]{1,0:T(8,128)(2,1)S(1)} copy-done((bf16[64,3200]{1,0:T(8,128)(2,1)S(1)}, bf16[64,3200]{1,0:T(8,128)(2,1)}, u32[]{:S(2)}) %copy-start.2) | copy-done | bytes 409624
  9.0 2.9 %collective-permute-start.1 = (bf16[16,3200]{1,0:T(8,128)(2,1)S(1)}, bf16[16,3200]{1,0:T(8,128)(2,1)S(1)}, u32[]{:S(2)}, u32[]{:S(2)}) collective-permute-start(bf16[16,3200]{1,0:T(8,128)(2,1)S(1)} %get-tuple-element.34), channel_id=1, source_target_pairs={{0,2},{1,3},{2,0},{3,1},{16,18},{17,19},{18,16},{19,17},{4,6},{5,7... | collective-permute-start | bytes 307208 | tf_op jit(solution)/shard_map/ppermute | solution.py:20
  11.9 1.5 %collective-permute-start.2 = (bf16[16,3200]{1,0:T(8,128)(2,1)S(1)}, bf16[16,3200]{1,0:T(8,128)(2,1)S(1)}, u32[]{:S(2)}, u32[]{:S(2)}) collective-permute-start(bf16[16,3200]{1,0:T(8,128)(2,1)S(1)} %get-tuple-element.35), channel_id=1, source_target_pairs={{0,16},{1,17},{2,18},{3,19},{16,0},{17,1},{18,2},{19,3},{4,20},{5,... | collective-permute-start | bytes 307208 | tf_op jit(solution)/shard_map/ppermute | solution.py:20
  13.5 5.0 %near.1 = (bf16[3072,2304]{1,0:T(8,128)(2,1)S(1)}, f32[8,128]{1,0:T(8,128)S(1)}) custom-call(f32[16,3200]{1,0:T(8,128)S(1)} %get-tuple-element.31.after_ref.own_ref, bf16[3072,2304]{1,0:T(8,128)(2,1)} %source_ref.1), custom_call_target="tpu_custom_call" | custom-call | bytes 28311552 | tf_op jit(solution)/shard_map/near/pallas_call | solution.py:155
  19.1 2.7 %collective-permute-start.4 = (bf16[4,3200]{1,0:T(4,128)(2,1)S(1)}, bf16[4,3200]{1,0:T(4,128)(2,1)S(1)}, u32[]{:S(2)}, u32[]{:S(2)}) collective-permute-start(bf16[4,3200]{1,0:T(4,128)(2,1)S(1)} %get-tuple-element.38), channel_id=1, source_target_pairs={{0,8},{4,12},{8,0},{12,4},{1,9},{5,13},{9,1},{13,5},{2,10},{6,14},... | collective-permute-start | bytes 76808 | tf_op jit(solution)/shard_map/ppermute | solution.py:20
  21.8 1.4 %collective-permute-start.5 = (bf16[4,3200]{1,0:T(4,128)(2,1)S(1)}, bf16[4,3200]{1,0:T(4,128)(2,1)S(1)}, u32[]{:S(2)}, u32[]{:S(2)}) collective-permute-start(bf16[4,3200]{1,0:T(4,128)(2,1)S(1)} %get-tuple-element.39), channel_id=1, source_target_pairs={{0,12},{4,8},{8,4},{12,0},{1,13},{5,9},{9,5},{13,1},{2,14},{6,10},... | collective-permute-start | bytes 76808 | tf_op jit(solution)/shard_map/ppermute | solution.py:20
  23.9 3.5 %collective-permute-done.5.refs_2_ = bf16[4,3200]{1,0:T(4,128)(2,1)S(1)} collective-permute-done((bf16[4,3200]{1,0:T(4,128)(2,1)S(1)}, bf16[4,3200]{1,0:T(4,128)(2,1)S(1)}, u32[]{:S(2)}, u32[]{:S(2)}) %collective-permute-start.5) | collective-permute-done | bytes 25632 | tf_op jit(solution)/shard_map/ppermute | solution.py:20
  27.4 1.8 %attend.1 = (bf16[4,3072]{1,0:T(4,128)(2,1)S(1)}, bf16[4,3072]{1,0:T(4,128)(2,1)S(1)}, bf16[4,3072]{1,0:T(4,128)(2,1)S(1)}, bf16[4,3072]{1,0:T(4,128)(2,1)S(1)}) custom-call(f32[2,1,2048]{2,1,0:T(1,128)S(1)} %compare_select_fusion.mask_ref, f32[2,2,128]{2,1,0:T(2,128)S(1)} %get-tuple-element.54.cos_ref, f32[2,2,128]{2,1,0:T(2,128)S(1)} %get-tuple-element.53.sin_ref, ...), custom_call_target="tpu_custom_call" | custom-call | flops 402653184 | bytes 4194304 | tf_op jit(solution)/shard_map/attend/pallas_call | solution.py:319
  29.2 1.3 %collective-permute-start.7 = (bf16[4,3072]{1,0:T(4,128)(2,1)S(1)}, bf16[4,3072]{1,0:T(4,128)(2,1)S(1)}, u32[]{:S(2)}, u32[]{:S(2)}) collective-permute-start(bf16[4,3072]{1,0:T(4,128)(2,1)S(1)} %get-tuple-element.42), channel_id=1, source_target_pairs={{0,8},{4,12},{8,0},{12,4},{1,9},{5,13},{9,1},{13,5},{2,10},{6,14},... | collective-permute-start | bytes 73736 | tf_op jit(solution)/shard_map/ppermute | solution.py:20
  31.5 1.3 %collective-permute-start.9 = (bf16[4,3072]{1,0:T(4,128)(2,1)S(1)}, bf16[4,3072]{1,0:T(4,128)(2,1)S(1)}, u32[]{:S(2)}, u32[]{:S(2)}) collective-permute-start(bf16[4,3072]{1,0:T(4,128)(2,1)S(1)} %get-tuple-element.44), channel_id=1, source_target_pairs={{0,4},{4,0},{8,12},{12,8},{1,5},{5,1},{9,13},{13,9},{2,6},{6,2},{1... | collective-permute-start | bytes 73736 | tf_op jit(solution)/shard_map/ppermute | solution.py:20
  32.8 1.2 %collective-permute-done.7.refs_1_ = bf16[4,3072]{1,0:T(4,128)(2,1)S(1)} collective-permute-done((bf16[4,3072]{1,0:T(4,128)(2,1)S(1)}, bf16[4,3072]{1,0:T(4,128)(2,1)S(1)}, u32[]{:S(2)}, u32[]{:S(2)}) %collective-permute-start.7) | collective-permute-done | bytes 24608 | tf_op jit(solution)/shard_map/ppermute | solution.py:20
  34.0 2.1 %collective-permute-done.8.refs_2_ = bf16[4,3072]{1,0:T(4,128)(2,1)S(1)} collective-permute-done((bf16[4,3072]{1,0:T(4,128)(2,1)S(1)}, bf16[4,3072]{1,0:T(4,128)(2,1)S(1)}, u32[]{:S(2)}, u32[]{:S(2)}) %collective-permute-start.8) | collective-permute-done | bytes 24608 | tf_op jit(solution)/shard_map/ppermute | solution.py:20
  36.3 2.5 %collective-permute-start.10 = (bf16[16,3072]{1,0:T(8,128)(2,1)S(1)}, bf16[16,3072]{1,0:T(8,128)(2,1)S(1)}, u32[]{:S(2)}, u32[]{:S(2)}) collective-permute-start(bf16[16,3072]{1,0:T(8,128)(2,1)S(1)} %order.1.refs_7_), channel_id=1, source_target_pairs={{0,18},{1,19},{2,16},{3,17},{16,2},{17,3},{18,0},{19,1},{4,22},{5,... | collective-permute-start | bytes 294920 | tf_op jit(solution)/shard_map/ppermute | solution.py:20
  39.8 2.0 %collective-permute-done.10.refs_4_ = bf16[16,3072]{1,0:T(8,128)(2,1)S(1)} collective-permute-done((bf16[16,3072]{1,0:T(8,128)(2,1)S(1)}, bf16[16,3072]{1,0:T(8,128)(2,1)S(1)}, u32[]{:S(2)}, u32[]{:S(2)}) %collective-permute-start.10) | collective-permute-done | bytes 98336 | tf_op jit(solution)/shard_map/ppermute | solution.py:20
  41.8 1.5 %collective-permute-done.12.refs_5_ = bf16[16,3072]{1,0:T(8,128)(2,1)S(1)} collective-permute-done((bf16[16,3072]{1,0:T(8,128)(2,1)S(1)}, bf16[16,3072]{1,0:T(8,128)(2,1)S(1)}, u32[]{:S(2)}, u32[]{:S(2)}) %collective-permute-start.12) | collective-permute-done | bytes 98336 | tf_op jit(solution)/shard_map/ppermute | solution.py:20
  45.2 1.3 %mix.2 = (f32[32,1152]{1,0:T(8,128)S(1)}, bf16[32,1152]{1,0:T(8,128)(2,1)S(1)}, f32[32,1152]{1,0:T(8,128)S(1)}, bf16[32,1152]{1,0:T(8,128)(2,1)S(1)}) custom-call(bf16[3072,2304]{1,0:T(8,128)(2,1)S(1)} %get-tuple-element.32.weight_ref, bf16[16,3072]{1,0:T(8,128)(2,1)S(1)} %collective-permute-done.11.refs_0_, ...), custom_call_target="tpu_custom_call" | custom-call | flops 905969664 | bytes 7077888 | tf_op jit(solution)/shard_map/mix/pallas_call | solution.py:402
  47.0 1.3 %mix.3 = (f32[32,1152]{1,0:T(8,128)S(1)}, bf16[32,1152]{1,0:T(8,128)(2,1)S(1)}, f32[32,1152]{1,0:T(8,128)S(1)}, bf16[32,1152]{1,0:T(8,128)(2,1)S(1)}) custom-call(bf16[3072,2304]{1,0:T(8,128)(2,1)S(1)} %get-tuple-element.32.weight_ref, bf16[16,3072]{1,0:T(8,128)(2,1)S(1)} %collective-permute-done.11.refs_0_, ...), custom_call_target="tpu_custom_call" | custom-call | flops 905969664 | bytes 7077888 | tf_op jit(solution)/shard_map/mix/pallas_call | solution.py:402
  48.3 1.6 %collective-permute-start.19 = (bf16[32,1152]{1,0:T(8,128)(2,1)S(1)}, bf16[32,1152]{1,0:T(8,128)(2,1)S(1)}, u32[]{:S(2)}, u32[]{:S(2)}) collective-permute-start(bf16[32,1152]{1,0:T(8,128)(2,1)S(1)} %get-tuple-element.49), channel_id=1, source_target_pairs={{0,4},{4,0},{8,12},{12,8},{1,5},{5,1},{9,13},{13,9},{2,6},{6,2},{1... | collective-permute-start | bytes 221192 | tf_op jit(solution)/shard_map/ppermute | solution.py:20
  49.9 1.1 %collective-permute-done.17.taken_ref = bf16[32,1152]{1,0:T(8,128)(2,1)S(1)} collective-permute-done((bf16[32,1152]{1,0:T(8,128)(2,1)S(1)}, bf16[32,1152]{1,0:T(8,128)(2,1)S(1)}, u32[]{:S(2)}, u32[]{:S(2)}) %collective-permute-start.17) | collective-permute-done | bytes 73760 | tf_op jit(solution)/shard_map/ppermute | solution.py:20
  51.1 1.0 %collective-permute-start.18 = (bf16[32,1152]{1,0:T(8,128)(2,1)S(1)}, bf16[32,1152]{1,0:T(8,128)(2,1)S(1)}, u32[]{:S(2)}, u32[]{:S(2)}) collective-permute-start(bf16[32,1152]{1,0:T(8,128)(2,1)S(1)} %relay.3), channel_id=1, source_target_pairs={{0,8},{4,12},{8,0},{12,4},{1,9},{5,13},{9,1},{13,5},{2,10},{6,14},... | collective-permute-start | bytes 221192 | tf_op jit(solution)/shard_map/ppermute | solution.py:20
  52.7 2.9 %collective-permute-start.21 = (bf16[32,1152]{1,0:T(8,128)(2,1)S(1)}, bf16[32,1152]{1,0:T(8,128)(2,1)S(1)}, u32[]{:S(2)}, u32[]{:S(2)}) collective-permute-start(bf16[32,1152]{1,0:T(8,128)(2,1)S(1)} %relay.5.after_ref), channel_id=1, source_target_pairs={{0,8},{4,12},{8,0},{12,4},{1,9},{5,13},{9,1},{13,5},{2,10},{6,14},... | collective-permute-start | bytes 221192 | tf_op jit(solution)/shard_map/ppermute | solution.py:20
  55.6 2.0 %collective-permute-start.22 = (bf16[32,1152]{1,0:T(8,128)(2,1)S(1)}, bf16[32,1152]{1,0:T(8,128)(2,1)S(1)}, u32[]{:S(2)}, u32[]{:S(2)}) collective-permute-start(bf16[32,1152]{1,0:T(8,128)(2,1)S(1)} %held.3), channel_id=1, source_target_pairs={{0,4},{4,0},{8,12},{12,8},{1,5},{5,1},{9,13},{13,9},{2,6},{6,2},{1... | collective-permute-start | bytes 221192 | tf_op jit(solution)/shard_map/ppermute | solution.py:20
  58.4 2.0 %collective-permute-done.20.refs_1_ = bf16[32,1152]{1,0:T(8,128)(2,1)S(1)} collective-permute-done((bf16[32,1152]{1,0:T(8,128)(2,1)S(1)}, bf16[32,1152]{1,0:T(8,128)(2,1)S(1)}, u32[]{:S(2)}, u32[]{:S(2)}) %collective-permute-start.20) | collective-permute-done | bytes 73760 | tf_op jit(solution)/shard_map/ppermute | solution.py:20
  (49 shorter events, 9.8 us)
Async XLA Ops:
  6.8 20.6 %copy-start = (bf16[2,2048,256]{2,1,0:T(8,128)(2,1)S(1)}, bf16[2,2048,256]{2,1,0:T(8,128)(2,1)}, u32[]{:S(2)}) copy-start(bf16[2,2048,256]{2,1,0:T(8,128)(2,1)} %keys_ref.1) | copy-start | bytes 6291460
  6.8 2.1 %collective-permute-start = (bf16[64,3200]{1,0:T(8,128)(2,1)}, bf16[64,3200]{1,0:T(8,128)(2,1)S(1)}, u32[]{:S(2)}, u32[]{:S(2)}) collective-permute-start(bf16[64,3200]{1,0:T(8,128)(2,1)} %get-tuple-element.30), channel_id=1, source_target_pairs={{0,1},{1,0},{2,3},{3,2},{16,17},{17,16},{18,19},{19,18},{4,5},{5,4... | collective-permute-start | bytes 1228808 | tf_op jit(solution)/shard_map/ppermute | solution.py:20
  9.0 9.5 %collective-permute-start.1 = (bf16[16,3200]{1,0:T(8,128)(2,1)S(1)}, bf16[16,3200]{1,0:T(8,128)(2,1)S(1)}, u32[]{:S(2)}, u32[]{:S(2)}) collective-permute-start(bf16[16,3200]{1,0:T(8,128)(2,1)S(1)} %get-tuple-element.34), channel_id=1, source_target_pairs={{0,2},{1,3},{2,0},{3,1},{16,18},{17,19},{18,16},{19,17},{4,6},{5,7... | collective-permute-start | bytes 307208 | tf_op jit(solution)/shard_map/ppermute | solution.py:20
  11.9 6.6 %collective-permute-start.2 = (bf16[16,3200]{1,0:T(8,128)(2,1)S(1)}, bf16[16,3200]{1,0:T(8,128)(2,1)S(1)}, u32[]{:S(2)}, u32[]{:S(2)}) collective-permute-start(bf16[16,3200]{1,0:T(8,128)(2,1)S(1)} %get-tuple-element.35), channel_id=1, source_target_pairs={{0,16},{1,17},{2,18},{3,19},{16,0},{17,1},{18,2},{19,3},{4,20},{5,... | collective-permute-start | bytes 307208 | tf_op jit(solution)/shard_map/ppermute | solution.py:20
  13.5 5.6 %collective-permute-start.3 = (bf16[16,3200]{1,0:T(8,128)(2,1)S(1)}, bf16[16,3200]{1,0:T(8,128)(2,1)S(1)}, u32[]{:S(2)}, u32[]{:S(2)}) collective-permute-start(bf16[16,3200]{1,0:T(8,128)(2,1)S(1)} %get-tuple-element.36), channel_id=1, source_target_pairs={{0,18},{1,19},{2,16},{3,17},{16,2},{17,3},{18,0},{19,1},{4,22},{5,... | collective-permute-start | bytes 307208 | tf_op jit(solution)/shard_map/ppermute | solution.py:20
  19.1 4.8 %collective-permute-start.4 = (bf16[4,3200]{1,0:T(4,128)(2,1)S(1)}, bf16[4,3200]{1,0:T(4,128)(2,1)S(1)}, u32[]{:S(2)}, u32[]{:S(2)}) collective-permute-start(bf16[4,3200]{1,0:T(4,128)(2,1)S(1)} %get-tuple-element.38), channel_id=1, source_target_pairs={{0,8},{4,12},{8,0},{12,4},{1,9},{5,13},{9,1},{13,5},{2,10},{6,14},... | collective-permute-start | bytes 76808 | tf_op jit(solution)/shard_map/ppermute | solution.py:20
  21.8 5.6 %collective-permute-start.5 = (bf16[4,3200]{1,0:T(4,128)(2,1)S(1)}, bf16[4,3200]{1,0:T(4,128)(2,1)S(1)}, u32[]{:S(2)}, u32[]{:S(2)}) collective-permute-start(bf16[4,3200]{1,0:T(4,128)(2,1)S(1)} %get-tuple-element.39), channel_id=1, source_target_pairs={{0,12},{4,8},{8,4},{12,0},{1,13},{5,9},{9,5},{13,1},{2,14},{6,10},... | collective-permute-start | bytes 76808 | tf_op jit(solution)/shard_map/ppermute | solution.py:20
  23.1 4.3 %collective-permute-start.6 = (bf16[4,3200]{1,0:T(4,128)(2,1)S(1)}, bf16[4,3200]{1,0:T(4,128)(2,1)S(1)}, u32[]{:S(2)}, u32[]{:S(2)}) collective-permute-start(bf16[4,3200]{1,0:T(4,128)(2,1)S(1)} %get-tuple-element.40), channel_id=1, source_target_pairs={{0,4},{4,0},{8,12},{12,8},{1,5},{5,1},{9,13},{13,9},{2,6},{6,2},{1... | collective-permute-start | bytes 76808 | tf_op jit(solution)/shard_map/ppermute | solution.py:20
  29.2 4.8 %collective-permute-start.7 = (bf16[4,3072]{1,0:T(4,128)(2,1)S(1)}, bf16[4,3072]{1,0:T(4,128)(2,1)S(1)}, u32[]{:S(2)}, u32[]{:S(2)}) collective-permute-start(bf16[4,3072]{1,0:T(4,128)(2,1)S(1)} %get-tuple-element.42), channel_id=1, source_target_pairs={{0,8},{4,12},{8,0},{12,4},{1,9},{5,13},{9,1},{13,5},{2,10},{6,14},... | collective-permute-start | bytes 73736 | tf_op jit(solution)/shard_map/ppermute | solution.py:20
  30.6 5.6 %collective-permute-start.8 = (bf16[4,3072]{1,0:T(4,128)(2,1)S(1)}, bf16[4,3072]{1,0:T(4,128)(2,1)S(1)}, u32[]{:S(2)}, u32[]{:S(2)}) collective-permute-start(bf16[4,3072]{1,0:T(4,128)(2,1)S(1)} %get-tuple-element.43), channel_id=1, source_target_pairs={{0,12},{4,8},{8,4},{12,0},{1,13},{5,9},{9,5},{13,1},{2,14},{6,10},... | collective-permute-start | bytes 73736 | tf_op jit(solution)/shard_map/ppermute | solution.py:20
  31.5 4.7 %collective-permute-start.9 = (bf16[4,3072]{1,0:T(4,128)(2,1)S(1)}, bf16[4,3072]{1,0:T(4,128)(2,1)S(1)}, u32[]{:S(2)}, u32[]{:S(2)}) collective-permute-start(bf16[4,3072]{1,0:T(4,128)(2,1)S(1)} %get-tuple-element.44), channel_id=1, source_target_pairs={{0,4},{4,0},{8,12},{12,8},{1,5},{5,1},{9,13},{13,9},{2,6},{6,2},{1... | collective-permute-start | bytes 73736 | tf_op jit(solution)/shard_map/ppermute | solution.py:20
  36.3 5.6 %collective-permute-start.10 = (bf16[16,3072]{1,0:T(8,128)(2,1)S(1)}, bf16[16,3072]{1,0:T(8,128)(2,1)S(1)}, u32[]{:S(2)}, u32[]{:S(2)}) collective-permute-start(bf16[16,3072]{1,0:T(8,128)(2,1)S(1)} %order.1.refs_7_), channel_id=1, source_target_pairs={{0,18},{1,19},{2,16},{3,17},{16,2},{17,3},{18,0},{19,1},{4,22},{5,... | collective-permute-start | bytes 294920 | tf_op jit(solution)/shard_map/ppermute | solution.py:20
  38.8 4.6 %collective-permute-start.12 = (bf16[16,3072]{1,0:T(8,128)(2,1)S(1)}, bf16[16,3072]{1,0:T(8,128)(2,1)S(1)}, u32[]{:S(2)}, u32[]{:S(2)}) collective-permute-start(bf16[16,3072]{1,0:T(8,128)(2,1)S(1)} %order.1.refs_7_), channel_id=1, source_target_pairs={{0,16},{1,17},{2,18},{3,19},{16,0},{17,1},{18,2},{19,3},{4,20},{5,... | collective-permute-start | bytes 294920 | tf_op jit(solution)/shard_map/ppermute | solution.py:20
  39.3 4.6 %collective-permute-start.14 = (bf16[16,3072]{1,0:T(8,128)(2,1)S(1)}, bf16[16,3072]{1,0:T(8,128)(2,1)S(1)}, u32[]{:S(2)}, u32[]{:S(2)}) collective-permute-start(bf16[16,3072]{1,0:T(8,128)(2,1)S(1)} %order.1.refs_7_), channel_id=1, source_target_pairs={{0,2},{1,3},{2,0},{3,1},{16,18},{17,19},{18,16},{19,17},{4,6},{5,7... | collective-permute-start | bytes 294920 | tf_op jit(solution)/shard_map/ppermute | solution.py:20
  39.8 4.1 %collective-permute-start.16 = (bf16[16,3072]{1,0:T(8,128)(2,1)S(1)}, bf16[16,3072]{1,0:T(8,128)(2,1)S(1)}, u32[]{:S(2)}, u32[]{:S(2)}) collective-permute-start(bf16[16,3072]{1,0:T(8,128)(2,1)S(1)} %order.1.refs_7_), channel_id=1, source_target_pairs={{0,1},{1,0},{2,3},{3,2},{16,17},{17,16},{18,19},{19,18},{4,5},{5,4... | collective-permute-start | bytes 294920 | tf_op jit(solution)/shard_map/ppermute | solution.py:20
  41.8 2.1 %collective-permute-start.11 = (bf16[16,3072]{1,0:T(8,128)(2,1)S(1)}, bf16[16,3072]{1,0:T(8,128)(2,1)S(1)}, u32[]{:S(2)}, u32[]{:S(2)}) collective-permute-start(bf16[16,3072]{1,0:T(8,128)(2,1)S(1)} %collective-permute-done.10.refs_4_), channel_id=1, source_target_pairs={{0,1},{1,0},{2,3},{3,2},{16,17},{17,16},{18,19},{19,18},{4,5},{5,4... | collective-permute-start | bytes 294920 | tf_op jit(solution)/shard_map/ppermute | solution.py:20
  43.4 1.3 %collective-permute-start.13 = (bf16[16,3072]{1,0:T(8,128)(2,1)S(1)}, bf16[16,3072]{1,0:T(8,128)(2,1)S(1)}, u32[]{:S(2)}, u32[]{:S(2)}) collective-permute-start(bf16[16,3072]{1,0:T(8,128)(2,1)S(1)} %collective-permute-done.12.refs_5_), channel_id=1, source_target_pairs={{0,1},{1,0},{2,3},{3,2},{16,17},{17,16},{18,19},{19,18},{4,5},{5,4... | collective-permute-start | bytes 294920 | tf_op jit(solution)/shard_map/ppermute | solution.py:20
  43.9 1.3 %collective-permute-start.15 = (bf16[16,3072]{1,0:T(8,128)(2,1)S(1)}, bf16[16,3072]{1,0:T(8,128)(2,1)S(1)}, u32[]{:S(2)}, u32[]{:S(2)}) collective-permute-start(bf16[16,3072]{1,0:T(8,128)(2,1)S(1)} %collective-permute-done.14.refs_6_), channel_id=1, source_target_pairs={{0,1},{1,0},{2,3},{3,2},{16,17},{17,16},{18,19},{19,18},{4,5},{5,4... | collective-permute-start | bytes 294920 | tf_op jit(solution)/shard_map/ppermute | solution.py:20
  46.5 4.5 %collective-permute-start.17 = (bf16[32,1152]{1,0:T(8,128)(2,1)S(1)}, bf16[32,1152]{1,0:T(8,128)(2,1)S(1)}, u32[]{:S(2)}, u32[]{:S(2)}) collective-permute-start(bf16[32,1152]{1,0:T(8,128)(2,1)S(1)} %get-tuple-element.47), channel_id=1, source_target_pairs={{0,4},{4,0},{8,12},{12,8},{1,5},{5,1},{9,13},{13,9},{2,6},{6,2},{1... | collective-permute-start | bytes 221192 | tf_op jit(solution)/shard_map/ppermute | solution.py:20
  48.3 4.4 %collective-permute-start.19 = (bf16[32,1152]{1,0:T(8,128)(2,1)S(1)}, bf16[32,1152]{1,0:T(8,128)(2,1)S(1)}, u32[]{:S(2)}, u32[]{:S(2)}) collective-permute-start(bf16[32,1152]{1,0:T(8,128)(2,1)S(1)} %get-tuple-element.49), channel_id=1, source_target_pairs={{0,4},{4,0},{8,12},{12,8},{1,5},{5,1},{9,13},{13,9},{2,6},{6,2},{1... | collective-permute-start | bytes 221192 | tf_op jit(solution)/shard_map/ppermute | solution.py:20
  51.1 7.3 %collective-permute-start.18 = (bf16[32,1152]{1,0:T(8,128)(2,1)S(1)}, bf16[32,1152]{1,0:T(8,128)(2,1)S(1)}, u32[]{:S(2)}, u32[]{:S(2)}) collective-permute-start(bf16[32,1152]{1,0:T(8,128)(2,1)S(1)} %relay.3), channel_id=1, source_target_pairs={{0,8},{4,12},{8,0},{12,4},{1,9},{5,13},{9,1},{13,5},{2,10},{6,14},... | collective-permute-start | bytes 221192 | tf_op jit(solution)/shard_map/ppermute | solution.py:20
  52.7 7.7 %collective-permute-start.21 = (bf16[32,1152]{1,0:T(8,128)(2,1)S(1)}, bf16[32,1152]{1,0:T(8,128)(2,1)S(1)}, u32[]{:S(2)}, u32[]{:S(2)}) collective-permute-start(bf16[32,1152]{1,0:T(8,128)(2,1)S(1)} %relay.5.after_ref), channel_id=1, source_target_pairs={{0,8},{4,12},{8,0},{12,4},{1,9},{5,13},{9,1},{13,5},{2,10},{6,14},... | collective-permute-start | bytes 221192 | tf_op jit(solution)/shard_map/ppermute | solution.py:20
  55.6 4.8 %collective-permute-start.20 = (bf16[32,1152]{1,0:T(8,128)(2,1)S(1)}, bf16[32,1152]{1,0:T(8,128)(2,1)S(1)}, u32[]{:S(2)}, u32[]{:S(2)}) collective-permute-start(bf16[32,1152]{1,0:T(8,128)(2,1)S(1)} %held.2), channel_id=1, source_target_pairs={{0,4},{4,0},{8,12},{12,8},{1,5},{5,1},{9,13},{13,9},{2,6},{6,2},{1... | collective-permute-start | bytes 221192 | tf_op jit(solution)/shard_map/ppermute | solution.py:20
  55.6 5.5 %collective-permute-start.22 = (bf16[32,1152]{1,0:T(8,128)(2,1)S(1)}, bf16[32,1152]{1,0:T(8,128)(2,1)S(1)}, u32[]{:S(2)}, u32[]{:S(2)}) collective-permute-start(bf16[32,1152]{1,0:T(8,128)(2,1)S(1)} %held.3), channel_id=1, source_target_pairs={{0,4},{4,0},{8,12},{12,8},{1,5},{5,1},{9,13},{13,9},{2,6},{6,2},{1... | collective-permute-start | bytes 221192 | tf_op jit(solution)/shard_map/ppermute | solution.py:20
  (3 other events, 30.5 us)

commit v3 on v1

--- a/solution.py
+++ b/solution.py
@@ -272,12 +272,16 @@
                     window = pl.ds((k * heads + h) * steps, steps)
                     rows_ref[s, window, pl.ds(part * half, half)] = value[s * steps : (s + 1) * steps]
     step_of = lax.broadcasted_iota(jnp.int32, (count, 1), 0) % steps
+    all_queries = [rows_ref[s, pl.ds(0, count)].astype(jnp.bfloat16) for s in range(owned)]
+    scores = [
+        lax.dot_general(
+            all_queries[s], keys_ref[s], (((1,), (1,)), ((), ())), preferred_element_type=jnp.float32
+        )
+        for s in range(owned)
+    ]
     for s in range(owned):
-        queries = rows_ref[s, pl.ds(0, count)].astype(jnp.bfloat16)
-        cached = lax.dot_general(
-            queries, keys_ref[s], (((1,), (1,)), ((), ())), preferred_element_type=jnp.float32
-        )
-        cached = cached + mask_ref[s]
+        queries = all_queries[s]
+        cached = scores[s] + mask_ref[s]
         highest = cached.max(-1, keepdims=True)
         wide = queries.astype(jnp.float32)
         fresh = []

time: 61.4 us -> 61.4 us (level)
  no operation moved by 1% of the time
where the time goes in v3:
time: 61.4 us; the launch traced here: 61.2 us
  starting transfers between devices  23.6 us (38%)
  Pallas kernels  18 us (29%)
  waiting for transfers between devices  17.9 us (29%)
  local copies, waits for them, and re-layouts  1.28 us (2%)
    ppermute x23, starting transfers between devices, swapped_with(): return lax.ppermute(value, axes, pairs)  23.6 us
    ppermute x23, waiting for transfers between devices, swapped_with(): return lax.ppermute(value, axes, pairs)  17.9 us
    pallas_call x1, Pallas kernels, project(): pl.pallas_call(functools.partial(project_kernel, dims, blocks, chunks), o...  6.77 us
    pallas_call x1, Pallas kernels, near(): pl.pallas_call(near_kernel, out_shape=(jax.ShapeDtypeStruct(array.shape,...  5.04 us
    pallas_call x2, Pallas kernels, mix(): pl.pallas_call(functools.partial(mix_kernel, dims, chunk, part), out_shap...  2.58 us
    pallas_call x1, Pallas kernels, attend(): pl.pallas_call(functools.partial(attend_kernel, (gx_count, owned, steps,...  1.81 us
    pallas_call x2, Pallas kernels, finish(): pl.pallas_call(functools.partial(finish_kernel, dims), grid=(1,), out_sha...  1.46 us
    unnamed x8, local copies, waits for them, and re-layouts  1.28 us
  transfers between devices with their start and end apart: 23, of which 15 were waited for; matrix products, arithmetic and copies ran while one was open for 0% of the time, Pallas kernels for 12%

profile of v3, /device:TPU:0, one launch (start us, length us, event | category | flops | bytes accessed | tf_op | source)
XLA Modules:
  0.0 61.2 jit_solution(10367014301187563956)
XLA Ops:
  0.0 6.8 %project.1 = (bf16[64,3200]{1,0:T(8,128)(2,1)}, bf16[64,3200]{1,0:T(8,128)(2,1)}) custom-call(bf16[64,2,2304]{2,1,0:T(2,128)(2,1)} %tokens_hbm.1, bf16[2304,3072]{1,0:T(8,128)(2,1)} %query_hbm.1, bf16[2304,128]{1,0:T(8,128)(2,1)} %pair_hbm.1), custom_call_target="tpu_custom_call" | custom-call | flops 1887436800 | bytes 14745600 | tf_op jit(solution)/shard_map/project/pallas_call | solution.py:120
  7.3 1.3 %copy-done.2 = bf16[64,3200]{1,0:T(8,128)(2,1)S(1)} copy-done((bf16[64,3200]{1,0:T(8,128)(2,1)S(1)}, bf16[64,3200]{1,0:T(8,128)(2,1)}, u32[]{:S(2)}) %copy-start.2) | copy-done | bytes 409624
  9.0 2.9 %collective-permute-start.1 = (bf16[16,3200]{1,0:T(8,128)(2,1)S(1)}, bf16[16,3200]{1,0:T(8,128)(2,1)S(1)}, u32[]{:S(2)}, u32[]{:S(2)}) collective-permute-start(bf16[16,3200]{1,0:T(8,128)(2,1)S(1)} %get-tuple-element.38), channel_id=1, source_target_pairs={{0,2},{1,3},{2,0},{3,1},{16,18},{17,19},{18,16},{19,17},{4,6},{5,7... | collective-permute-start | bytes 307208 | tf_op jit(solution)/shard_map/ppermute | solution.py:20
  11.9 1.5 %collective-permute-start.2 = (bf16[16,3200]{1,0:T(8,128)(2,1)S(1)}, bf16[16,3200]{1,0:T(8,128)(2,1)S(1)}, u32[]{:S(2)}, u32[]{:S(2)}) collective-permute-start(bf16[16,3200]{1,0:T(8,128)(2,1)S(1)} %get-tuple-element.39), channel_id=1, source_target_pairs={{0,16},{1,17},{2,18},{3,19},{16,0},{17,1},{18,2},{19,3},{4,20},{5,... | collective-permute-start | bytes 307208 | tf_op jit(solution)/shard_map/ppermute | solution.py:20
  13.5 5.0 %near.1 = (bf16[3072,2304]{1,0:T(8,128)(2,1)S(1)}, f32[8,128]{1,0:T(8,128)S(1)}) custom-call(f32[16,3200]{1,0:T(8,128)S(1)} %get-tuple-element.35.after_ref.own_ref, bf16[3072,2304]{1,0:T(8,128)(2,1)} %source_ref.1), custom_call_target="tpu_custom_call" | custom-call | bytes 28311552 | tf_op jit(solution)/shard_map/near/pallas_call | solution.py:155
  19.1 2.7 %collective-permute-start.4 = (bf16[4,3200]{1,0:T(4,128)(2,1)S(1)}, bf16[4,3200]{1,0:T(4,128)(2,1)S(1)}, u32[]{:S(2)}, u32[]{:S(2)}) collective-permute-start(bf16[4,3200]{1,0:T(4,128)(2,1)S(1)} %get-tuple-element.42), channel_id=1, source_target_pairs={{0,8},{4,12},{8,0},{12,4},{1,9},{5,13},{9,1},{13,5},{2,10},{6,14},... | collective-permute-start | bytes 76808 | tf_op jit(solution)/shard_map/ppermute | solution.py:20
  21.8 1.4 %collective-permute-start.5 = (bf16[4,3200]{1,0:T(4,128)(2,1)S(1)}, bf16[4,3200]{1,0:T(4,128)(2,1)S(1)}, u32[]{:S(2)}, u32[]{:S(2)}) collective-permute-start(bf16[4,3200]{1,0:T(4,128)(2,1)S(1)} %get-tuple-element.43), channel_id=1, source_target_pairs={{0,12},{4,8},{8,4},{12,0},{1,13},{5,9},{9,5},{13,1},{2,14},{6,10},... | collective-permute-start | bytes 76808 | tf_op jit(solution)/shard_map/ppermute | solution.py:20
  23.9 3.5 %collective-permute-done.5.refs_2_ = bf16[4,3200]{1,0:T(4,128)(2,1)S(1)} collective-permute-done((bf16[4,3200]{1,0:T(4,128)(2,1)S(1)}, bf16[4,3200]{1,0:T(4,128)(2,1)S(1)}, u32[]{:S(2)}, u32[]{:S(2)}) %collective-permute-start.5) | collective-permute-done | bytes 25632 | tf_op jit(solution)/shard_map/ppermute | solution.py:20
  27.4 1.8 %attend.1 = (bf16[4,3072]{1,0:T(4,128)(2,1)S(1)}, bf16[4,3072]{1,0:T(4,128)(2,1)S(1)}, bf16[4,3072]{1,0:T(4,128)(2,1)S(1)}, bf16[4,3072]{1,0:T(4,128)(2,1)S(1)}) custom-call(f32[2,1,2048]{2,1,0:T(1,128)S(1)} %compare_select_fusion.mask_ref, f32[2,2,128]{2,1,0:T(2,128)S(1)} %get-tuple-element.62.cos_ref, f32[2,2,128]{2,1,0:T(2,128)S(1)} %get-tuple-element.61.sin_ref, ...), custom_call_target="tpu_custom_call" | custom-call | flops 402653184 | bytes 4194304 | tf_op jit(solution)/shard_map/attend/pallas_call | solution.py:323
  29.2 1.3 %collective-permute-start.7 = (bf16[4,3072]{1,0:T(4,128)(2,1)S(1)}, bf16[4,3072]{1,0:T(4,128)(2,1)S(1)}, u32[]{:S(2)}, u32[]{:S(2)}) collective-permute-start(bf16[4,3072]{1,0:T(4,128)(2,1)S(1)} %get-tuple-element.46), channel_id=1, source_target_pairs={{0,8},{4,12},{8,0},{12,4},{1,9},{5,13},{9,1},{13,5},{2,10},{6,14},... | collective-permute-start | bytes 73736 | tf_op jit(solution)/shard_map/ppermute | solution.py:20
  31.5 1.3 %collective-permute-start.9 = (bf16[4,3072]{1,0:T(4,128)(2,1)S(1)}, bf16[4,3072]{1,0:T(4,128)(2,1)S(1)}, u32[]{:S(2)}, u32[]{:S(2)}) collective-permute-start(bf16[4,3072]{1,0:T(4,128)(2,1)S(1)} %get-tuple-element.48), channel_id=1, source_target_pairs={{0,4},{4,0},{8,12},{12,8},{1,5},{5,1},{9,13},{13,9},{2,6},{6,2},{1... | collective-permute-start | bytes 73736 | tf_op jit(solution)/shard_map/ppermute | solution.py:20
  32.8 1.2 %collective-permute-done.7.refs_1_ = bf16[4,3072]{1,0:T(4,128)(2,1)S(1)} collective-permute-done((bf16[4,3072]{1,0:T(4,128)(2,1)S(1)}, bf16[4,3072]{1,0:T(4,128)(2,1)S(1)}, u32[]{:S(2)}, u32[]{:S(2)}) %collective-permute-start.7) | collective-permute-done | bytes 24608 | tf_op jit(solution)/shard_map/ppermute | solution.py:20
  34.0 2.1 %collective-permute-done.8.refs_2_ = bf16[4,3072]{1,0:T(4,128)(2,1)S(1)} collective-permute-done((bf16[4,3072]{1,0:T(4,128)(2,1)S(1)}, bf16[4,3072]{1,0:T(4,128)(2,1)S(1)}, u32[]{:S(2)}, u32[]{:S(2)}) %collective-permute-start.8) | collective-permute-done | bytes 24608 | tf_op jit(solution)/shard_map/ppermute | solution.py:20
  36.3 2.5 %collective-permute-start.10 = (bf16[16,3072]{1,0:T(8,128)(2,1)S(1)}, bf16[16,3072]{1,0:T(8,128)(2,1)S(1)}, u32[]{:S(2)}, u32[]{:S(2)}) collective-permute-start(bf16[16,3072]{1,0:T(8,128)(2,1)S(1)} %order.1.refs_7_), channel_id=1, source_target_pairs={{0,18},{1,19},{2,16},{3,17},{16,2},{17,3},{18,0},{19,1},{4,22},{5,... | collective-permute-start | bytes 294920 | tf_op jit(solution)/shard_map/ppermute | solution.py:20
  39.8 2.0 %collective-permute-done.10.refs_4_ = bf16[16,3072]{1,0:T(8,128)(2,1)S(1)} collective-permute-done((bf16[16,3072]{1,0:T(8,128)(2,1)S(1)}, bf16[16,3072]{1,0:T(8,128)(2,1)S(1)}, u32[]{:S(2)}, u32[]{:S(2)}) %collective-permute-start.10) | collective-permute-done | bytes 98336 | tf_op jit(solution)/shard_map/ppermute | solution.py:20
  41.8 1.5 %collective-permute-done.12.refs_5_ = bf16[16,3072]{1,0:T(8,128)(2,1)S(1)} collective-permute-done((bf16[16,3072]{1,0:T(8,128)(2,1)S(1)}, bf16[16,3072]{1,0:T(8,128)(2,1)S(1)}, u32[]{:S(2)}, u32[]{:S(2)}) %collective-permute-start.12) | collective-permute-done | bytes 98336 | tf_op jit(solution)/shard_map/ppermute | solution.py:20
  45.2 1.3 %mix.3 = (f32[32,1152]{1,0:T(8,128)S(1)}, bf16[32,1152]{1,0:T(8,128)(2,1)S(1)}, f32[32,1152]{1,0:T(8,128)S(1)}, bf16[32,1152]{1,0:T(8,128)(2,1)S(1)}) custom-call(bf16[3072,2304]{1,0:T(8,128)(2,1)S(1)} %get-tuple-element.36.weight_ref, bf16[16,3072]{1,0:T(8,128)(2,1)S(1)} %collective-permute-done.11.refs_0_, ...), custom_call_target="tpu_custom_call" | custom-call | flops 905969664 | bytes 7077888 | tf_op jit(solution)/shard_map/mix/pallas_call | solution.py:406
  47.0 1.3 %mix.2 = (f32[32,1152]{1,0:T(8,128)S(1)}, bf16[32,1152]{1,0:T(8,128)(2,1)S(1)}, f32[32,1152]{1,0:T(8,128)S(1)}, bf16[32,1152]{1,0:T(8,128)(2,1)S(1)}) custom-call(bf16[3072,2304]{1,0:T(8,128)(2,1)S(1)} %get-tuple-element.36.weight_ref, bf16[16,3072]{1,0:T(8,128)(2,1)S(1)} %collective-permute-done.11.refs_0_, ...), custom_call_target="tpu_custom_call" | custom-call | flops 905969664 | bytes 7077888 | tf_op jit(solution)/shard_map/mix/pallas_call | solution.py:406
  48.3 1.6 %collective-permute-start.17 = (bf16[32,1152]{1,0:T(8,128)(2,1)S(1)}, bf16[32,1152]{1,0:T(8,128)(2,1)S(1)}, u32[]{:S(2)}, u32[]{:S(2)}) collective-permute-start(bf16[32,1152]{1,0:T(8,128)(2,1)S(1)} %get-tuple-element.51), channel_id=1, source_target_pairs={{0,4},{4,0},{8,12},{12,8},{1,5},{5,1},{9,13},{13,9},{2,6},{6,2},{1... | collective-permute-start | bytes 221192 | tf_op jit(solution)/shard_map/ppermute | solution.py:20
  49.9 1.1 %collective-permute-done.20.taken_ref = bf16[32,1152]{1,0:T(8,128)(2,1)S(1)} collective-permute-done((bf16[32,1152]{1,0:T(8,128)(2,1)S(1)}, bf16[32,1152]{1,0:T(8,128)(2,1)S(1)}, u32[]{:S(2)}, u32[]{:S(2)}) %collective-permute-start.20) | collective-permute-done | bytes 73760 | tf_op jit(solution)/shard_map/ppermute | solution.py:20
  51.1 1.0 %collective-permute-start.21 = (bf16[32,1152]{1,0:T(8,128)(2,1)S(1)}, bf16[32,1152]{1,0:T(8,128)(2,1)S(1)}, u32[]{:S(2)}, u32[]{:S(2)}) collective-permute-start(bf16[32,1152]{1,0:T(8,128)(2,1)S(1)} %get-tuple-element.59), channel_id=1, source_target_pairs={{0,8},{4,12},{8,0},{12,4},{1,9},{5,13},{9,1},{13,5},{2,10},{6,14},... | collective-permute-start | bytes 221192 | tf_op jit(solution)/shard_map/ppermute | solution.py:20
  52.0 1.7 %collective-permute-start.22 = (bf16[32,1152]{1,0:T(8,128)(2,1)S(1)}, bf16[32,1152]{1,0:T(8,128)(2,1)S(1)}, u32[]{:S(2)}, u32[]{:S(2)}) collective-permute-start(bf16[32,1152]{1,0:T(8,128)(2,1)S(1)} %get-tuple-element.60), channel_id=1, source_target_pairs={{0,4},{4,0},{8,12},{12,8},{1,5},{5,1},{9,13},{13,9},{2,6},{6,2},{1... | collective-permute-start | bytes 221192 | tf_op jit(solution)/shard_map/ppermute | solution.py:20
  53.7 2.0 %collective-permute-start.18 = (bf16[32,1152]{1,0:T(8,128)(2,1)S(1)}, bf16[32,1152]{1,0:T(8,128)(2,1)S(1)}, u32[]{:S(2)}, u32[]{:S(2)}) collective-permute-start(bf16[32,1152]{1,0:T(8,128)(2,1)S(1)} %get-tuple-element.53), channel_id=1, source_target_pairs={{0,8},{4,12},{8,0},{12,4},{1,9},{5,13},{9,1},{13,5},{2,10},{6,14},... | collective-permute-start | bytes 221192 | tf_op jit(solution)/shard_map/ppermute | solution.py:20
  56.2 2.5 %collective-permute-done.21.refs_0_ = bf16[32,1152]{1,0:T(8,128)(2,1)S(1)} collective-permute-done((bf16[32,1152]{1,0:T(8,128)(2,1)S(1)}, bf16[32,1152]{1,0:T(8,128)(2,1)S(1)}, u32[]{:S(2)}, u32[]{:S(2)}) %collective-permute-start.21) | collective-permute-done | bytes 73760 | tf_op jit(solution)/shard_map/ppermute | solution.py:20
  (47 shorter events, 9.7 us)
Async XLA Ops:
  6.8 20.6 %copy-start = (bf16[2,2048,256]{2,1,0:T(8,128)(2,1)S(1)}, bf16[2,2048,256]{2,1,0:T(8,128)(2,1)}, u32[]{:S(2)}) copy-start(bf16[2,2048,256]{2,1,0:T(8,128)(2,1)} %keys_ref.1) | copy-start | bytes 6291460
  6.8 2.1 %collective-permute-start = (bf16[64,3200]{1,0:T(8,128)(2,1)}, bf16[64,3200]{1,0:T(8,128)(2,1)S(1)}, u32[]{:S(2)}, u32[]{:S(2)}) collective-permute-start(bf16[64,3200]{1,0:T(8,128)(2,1)} %get-tuple-element.34), channel_id=1, source_target_pairs={{0,1},{1,0},{2,3},{3,2},{16,17},{17,16},{18,19},{19,18},{4,5},{5,4... | collective-permute-start | bytes 1228808 | tf_op jit(solution)/shard_map/ppermute | solution.py:20
  9.0 9.5 %collective-permute-start.1 = (bf16[16,3200]{1,0:T(8,128)(2,1)S(1)}, bf16[16,3200]{1,0:T(8,128)(2,1)S(1)}, u32[]{:S(2)}, u32[]{:S(2)}) collective-permute-start(bf16[16,3200]{1,0:T(8,128)(2,1)S(1)} %get-tuple-element.38), channel_id=1, source_target_pairs={{0,2},{1,3},{2,0},{3,1},{16,18},{17,19},{18,16},{19,17},{4,6},{5,7... | collective-permute-start | bytes 307208 | tf_op jit(solution)/shard_map/ppermute | solution.py:20
  11.9 6.6 %collective-permute-start.2 = (bf16[16,3200]{1,0:T(8,128)(2,1)S(1)}, bf16[16,3200]{1,0:T(8,128)(2,1)S(1)}, u32[]{:S(2)}, u32[]{:S(2)}) collective-permute-start(bf16[16,3200]{1,0:T(8,128)(2,1)S(1)} %get-tuple-element.39), channel_id=1, source_target_pairs={{0,16},{1,17},{2,18},{3,19},{16,0},{17,1},{18,2},{19,3},{4,20},{5,... | collective-permute-start | bytes 307208 | tf_op jit(solution)/shard_map/ppermute | solution.py:20
  13.5 5.6 %collective-permute-start.3 = (bf16[16,3200]{1,0:T(8,128)(2,1)S(1)}, bf16[16,3200]{1,0:T(8,128)(2,1)S(1)}, u32[]{:S(2)}, u32[]{:S(2)}) collective-permute-start(bf16[16,3200]{1,0:T(8,128)(2,1)S(1)} %get-tuple-element.40), channel_id=1, source_target_pairs={{0,18},{1,19},{2,16},{3,17},{16,2},{17,3},{18,0},{19,1},{4,22},{5,... | collective-permute-start | bytes 307208 | tf_op jit(solution)/shard_map/ppermute | solution.py:20
  19.1 4.8 %collective-permute-start.4 = (bf16[4,3200]{1,0:T(4,128)(2,1)S(1)}, bf16[4,3200]{1,0:T(4,128)(2,1)S(1)}, u32[]{:S(2)}, u32[]{:S(2)}) collective-permute-start(bf16[4,3200]{1,0:T(4,128)(2,1)S(1)} %get-tuple-element.42), channel_id=1, source_target_pairs={{0,8},{4,12},{8,0},{12,4},{1,9},{5,13},{9,1},{13,5},{2,10},{6,14},... | collective-permute-start | bytes 76808 | tf_op jit(solution)/shard_map/ppermute | solution.py:20
  21.8 5.6 %collective-permute-start.5 = (bf16[4,3200]{1,0:T(4,128)(2,1)S(1)}, bf16[4,3200]{1,0:T(4,128)(2,1)S(1)}, u32[]{:S(2)}, u32[]{:S(2)}) collective-permute-start(bf16[4,3200]{1,0:T(4,128)(2,1)S(1)} %get-tuple-element.43), channel_id=1, source_target_pairs={{0,12},{4,8},{8,4},{12,0},{1,13},{5,9},{9,5},{13,1},{2,14},{6,10},... | collective-permute-start | bytes 76808 | tf_op jit(solution)/shard_map/ppermute | solution.py:20
  23.1 4.3 %collective-permute-start.6 = (bf16[4,3200]{1,0:T(4,128)(2,1)S(1)}, bf16[4,3200]{1,0:T(4,128)(2,1)S(1)}, u32[]{:S(2)}, u32[]{:S(2)}) collective-permute-start(bf16[4,3200]{1,0:T(4,128)(2,1)S(1)} %get-tuple-element.44), channel_id=1, source_target_pairs={{0,4},{4,0},{8,12},{12,8},{1,5},{5,1},{9,13},{13,9},{2,6},{6,2},{1... | collective-permute-start | bytes 76808 | tf_op jit(solution)/shard_map/ppermute | solution.py:20
  29.2 4.8 %collective-permute-start.7 = (bf16[4,3072]{1,0:T(4,128)(2,1)S(1)}, bf16[4,3072]{1,0:T(4,128)(2,1)S(1)}, u32[]{:S(2)}, u32[]{:S(2)}) collective-permute-start(bf16[4,3072]{1,0:T(4,128)(2,1)S(1)} %get-tuple-element.46), channel_id=1, source_target_pairs={{0,8},{4,12},{8,0},{12,4},{1,9},{5,13},{9,1},{13,5},{2,10},{6,14},... | collective-permute-start | bytes 73736 | tf_op jit(solution)/shard_map/ppermute | solution.py:20
  30.5 5.6 %collective-permute-start.8 = (bf16[4,3072]{1,0:T(4,128)(2,1)S(1)}, bf16[4,3072]{1,0:T(4,128)(2,1)S(1)}, u32[]{:S(2)}, u32[]{:S(2)}) collective-permute-start(bf16[4,3072]{1,0:T(4,128)(2,1)S(1)} %get-tuple-element.47), channel_id=1, source_target_pairs={{0,12},{4,8},{8,4},{12,0},{1,13},{5,9},{9,5},{13,1},{2,14},{6,10},... | collective-permute-start | bytes 73736 | tf_op jit(solution)/shard_map/ppermute | solution.py:20
  31.5 4.7 %collective-permute-start.9 = (bf16[4,3072]{1,0:T(4,128)(2,1)S(1)}, bf16[4,3072]{1,0:T(4,128)(2,1)S(1)}, u32[]{:S(2)}, u32[]{:S(2)}) collective-permute-start(bf16[4,3072]{1,0:T(4,128)(2,1)S(1)} %get-tuple-element.48), channel_id=1, source_target_pairs={{0,4},{4,0},{8,12},{12,8},{1,5},{5,1},{9,13},{13,9},{2,6},{6,2},{1... | collective-permute-start | bytes 73736 | tf_op jit(solution)/shard_map/ppermute | solution.py:20
  36.3 5.6 %collective-permute-start.10 = (bf16[16,3072]{1,0:T(8,128)(2,1)S(1)}, bf16[16,3072]{1,0:T(8,128)(2,1)S(1)}, u32[]{:S(2)}, u32[]{:S(2)}) collective-permute-start(bf16[16,3072]{1,0:T(8,128)(2,1)S(1)} %order.1.refs_7_), channel_id=1, source_target_pairs={{0,18},{1,19},{2,16},{3,17},{16,2},{17,3},{18,0},{19,1},{4,22},{5,... | collective-permute-start | bytes 294920 | tf_op jit(solution)/shard_map/ppermute | solution.py:20
  38.8 4.6 %collective-permute-start.12 = (bf16[16,3072]{1,0:T(8,128)(2,1)S(1)}, bf16[16,3072]{1,0:T(8,128)(2,1)S(1)}, u32[]{:S(2)}, u32[]{:S(2)}) collective-permute-start(bf16[16,3072]{1,0:T(8,128)(2,1)S(1)} %order.1.refs_7_), channel_id=1, source_target_pairs={{0,16},{1,17},{2,18},{3,19},{16,0},{17,1},{18,2},{19,3},{4,20},{5,... | collective-permute-start | bytes 294920 | tf_op jit(solution)/shard_map/ppermute | solution.py:20
  39.3 4.6 %collective-permute-start.14 = (bf16[16,3072]{1,0:T(8,128)(2,1)S(1)}, bf16[16,3072]{1,0:T(8,128)(2,1)S(1)}, u32[]{:S(2)}, u32[]{:S(2)}) collective-permute-start(bf16[16,3072]{1,0:T(8,128)(2,1)S(1)} %order.1.refs_7_), channel_id=1, source_target_pairs={{0,2},{1,3},{2,0},{3,1},{16,18},{17,19},{18,16},{19,17},{4,6},{5,7... | collective-permute-start | bytes 294920 | tf_op jit(solution)/shard_map/ppermute | solution.py:20
  39.8 4.1 %collective-permute-start.16 = (bf16[16,3072]{1,0:T(8,128)(2,1)S(1)}, bf16[16,3072]{1,0:T(8,128)(2,1)S(1)}, u32[]{:S(2)}, u32[]{:S(2)}) collective-permute-start(bf16[16,3072]{1,0:T(8,128)(2,1)S(1)} %order.1.refs_7_), channel_id=1, source_target_pairs={{0,1},{1,0},{2,3},{3,2},{16,17},{17,16},{18,19},{19,18},{4,5},{5,4... | collective-permute-start | bytes 294920 | tf_op jit(solution)/shard_map/ppermute | solution.py:20
  41.8 2.1 %collective-permute-start.11 = (bf16[16,3072]{1,0:T(8,128)(2,1)S(1)}, bf16[16,3072]{1,0:T(8,128)(2,1)S(1)}, u32[]{:S(2)}, u32[]{:S(2)}) collective-permute-start(bf16[16,3072]{1,0:T(8,128)(2,1)S(1)} %collective-permute-done.10.refs_4_), channel_id=1, source_target_pairs={{0,1},{1,0},{2,3},{3,2},{16,17},{17,16},{18,19},{19,18},{4,5},{5,4... | collective-permute-start | bytes 294920 | tf_op jit(solution)/shard_map/ppermute | solution.py:20
  43.4 1.3 %collective-permute-start.13 = (bf16[16,3072]{1,0:T(8,128)(2,1)S(1)}, bf16[16,3072]{1,0:T(8,128)(2,1)S(1)}, u32[]{:S(2)}, u32[]{:S(2)}) collective-permute-start(bf16[16,3072]{1,0:T(8,128)(2,1)S(1)} %collective-permute-done.12.refs_5_), channel_id=1, source_target_pairs={{0,1},{1,0},{2,3},{3,2},{16,17},{17,16},{18,19},{19,18},{4,5},{5,4... | collective-permute-start | bytes 294920 | tf_op jit(solution)/shard_map/ppermute | solution.py:20
  43.9 1.3 %collective-permute-start.15 = (bf16[16,3072]{1,0:T(8,128)(2,1)S(1)}, bf16[16,3072]{1,0:T(8,128)(2,1)S(1)}, u32[]{:S(2)}, u32[]{:S(2)}) collective-permute-start(bf16[16,3072]{1,0:T(8,128)(2,1)S(1)} %collective-permute-done.14.refs_6_), channel_id=1, source_target_pairs={{0,1},{1,0},{2,3},{3,2},{16,17},{17,16},{18,19},{19,18},{4,5},{5,4... | collective-permute-start | bytes 294920 | tf_op jit(solution)/shard_map/ppermute | solution.py:20
  46.5 4.5 %collective-permute-start.20 = (bf16[32,1152]{1,0:T(8,128)(2,1)S(1)}, bf16[32,1152]{1,0:T(8,128)(2,1)S(1)}, u32[]{:S(2)}, u32[]{:S(2)}) collective-permute-start(bf16[32,1152]{1,0:T(8,128)(2,1)S(1)} %get-tuple-element.57), channel_id=1, source_target_pairs={{0,4},{4,0},{8,12},{12,8},{1,5},{5,1},{9,13},{13,9},{2,6},{6,2},{1... | collective-permute-start | bytes 221192 | tf_op jit(solution)/shard_map/ppermute | solution.py:20
  48.3 5.4 %collective-permute-start.17 = (bf16[32,1152]{1,0:T(8,128)(2,1)S(1)}, bf16[32,1152]{1,0:T(8,128)(2,1)S(1)}, u32[]{:S(2)}, u32[]{:S(2)}) collective-permute-start(bf16[32,1152]{1,0:T(8,128)(2,1)S(1)} %get-tuple-element.51), channel_id=1, source_target_pairs={{0,4},{4,0},{8,12},{12,8},{1,5},{5,1},{9,13},{13,9},{2,6},{6,2},{1... | collective-permute-start | bytes 221192 | tf_op jit(solution)/shard_map/ppermute | solution.py:20
  51.1 7.7 %collective-permute-start.21 = (bf16[32,1152]{1,0:T(8,128)(2,1)S(1)}, bf16[32,1152]{1,0:T(8,128)(2,1)S(1)}, u32[]{:S(2)}, u32[]{:S(2)}) collective-permute-start(bf16[32,1152]{1,0:T(8,128)(2,1)S(1)} %get-tuple-element.59), channel_id=1, source_target_pairs={{0,8},{4,12},{8,0},{12,4},{1,9},{5,13},{9,1},{13,5},{2,10},{6,14},... | collective-permute-start | bytes 221192 | tf_op jit(solution)/shard_map/ppermute | solution.py:20
  52.0 6.7 %collective-permute-start.22 = (bf16[32,1152]{1,0:T(8,128)(2,1)S(1)}, bf16[32,1152]{1,0:T(8,128)(2,1)S(1)}, u32[]{:S(2)}, u32[]{:S(2)}) collective-permute-start(bf16[32,1152]{1,0:T(8,128)(2,1)S(1)} %get-tuple-element.60), channel_id=1, source_target_pairs={{0,4},{4,0},{8,12},{12,8},{1,5},{5,1},{9,13},{13,9},{2,6},{6,2},{1... | collective-permute-start | bytes 221192 | tf_op jit(solution)/shard_map/ppermute | solution.py:20
  53.7 6.6 %collective-permute-start.18 = (bf16[32,1152]{1,0:T(8,128)(2,1)S(1)}, bf16[32,1152]{1,0:T(8,128)(2,1)S(1)}, u32[]{:S(2)}, u32[]{:S(2)}) collective-permute-start(bf16[32,1152]{1,0:T(8,128)(2,1)S(1)} %get-tuple-element.53), channel_id=1, source_target_pairs={{0,8},{4,12},{8,0},{12,4},{1,9},{5,13},{9,1},{13,5},{2,10},{6,14},... | collective-permute-start | bytes 221192 | tf_op jit(solution)/shard_map/ppermute | solution.py:20
  55.7 4.8 %collective-permute-start.19 = (bf16[32,1152]{1,0:T(8,128)(2,1)S(1)}, bf16[32,1152]{1,0:T(8,128)(2,1)S(1)}, u32[]{:S(2)}, u32[]{:S(2)}) collective-permute-start(bf16[32,1152]{1,0:T(8,128)(2,1)S(1)} %get-tuple-element.54), channel_id=1, source_target_pairs={{0,4},{4,0},{8,12},{12,8},{1,5},{5,1},{9,13},{13,9},{2,6},{6,2},{1... | collective-permute-start | bytes 221192 | tf_op jit(solution)/shard_map/ppermute | solution.py:20
  (3 other events, 30.5 us)
